TPU v7x, 32 devices: a whole 2x2x4 slice. The times are simulated.
32 devices in a mesh: groups: 1, gx: 8 (over z, y), gy: 2 (over core), segment: 2 (over x).
Axes of the slice: x: 2, y: 2, z: 4, core: 2. Of those that a mesh axis runs over, the one named last changes fastest.
Arguments:
- activations: bfloat16 [2, 8, 128, 128, 128], P('segment', 'groups', 'gx', 'gy'), may hold values from -6 to 6
- cotangent: bfloat16 [8, 128, 128, 128], P('groups', 'gx', 'gy'), may hold values from -6 to 6
- spectral_weights: float32 [2, 32, 32, 8, 8, 32], P('segment', 'gy', 'gx'), may hold values from -6 to 6
- pointwise: float32 [2, 8, 8], P('segment'), may hold values from -2 to 2
- channel_bias: float32 [2, 8], P('segment'), may hold values from -3 to 3
Outputs:
- input_grads: bfloat16 [2, 8, 128, 128, 128], P('segment', 'groups', 'gx', 'gy')
- spectral_grads: float32 [2, 32, 32, 8, 8, 32], P('segment', 'gy', 'gx', 'groups')
All inputs are finite; a program needn't handle non-finite values.
Results may differ from a plain program's by a relative error of at most 0.0042.
Values may be sent and summed in bfloat16 or wider, within the bound.
A program may use at most 64 MiB of HBM per device.

v0:
```python
import functools
import math

import jax
import jax.numpy as jnp
import ml_dtypes
import numpy as np
from jax import lax
from jax.experimental import pallas as pl
from jax.experimental.pallas import tpu as pltpu
from jax.sharding import PartitionSpec as P

MODES = 32
f32, bf16 = jnp.float32, jnp.bfloat16


def from_behind(block, axis, distance):
    devices = range(lax.axis_size(axis))
    route = [(i - distance, i) for i in devices if i - distance in devices]
    return lax.ppermute(block, axis, route)


def trig_basis(length):
    half = MODES // 2
    freqs = np.arange(half)[:, None]
    points = np.arange(length)[None, :]
    step = 2.0 * math.pi / length
    rows = np.concatenate(
        [np.cos((freqs * points % length) * step), np.sin(((freqs + 1) * points % length) * step)]
    )
    scales = np.where(np.arange(MODES) == 0, 1.0 / math.sqrt(length), math.sqrt(2.0 / length))
    return rows * scales[:, None]


def halves(matrix):
    matrix = np.asarray(matrix, np.float32)
    top = matrix.astype(ml_dtypes.bfloat16)
    rest = (matrix - top.astype(np.float32)).astype(ml_dtypes.bfloat16)
    return np.stack([top, rest])


def split(value):
    top = value.astype(bf16)
    return top, (value - top.astype(f32)).astype(bf16)


def dot(a, b, ca=1, cb=0):
    return lax.dot_general(a, b, (((ca,), (cb,)), ((), ())), preferred_element_type=f32)


def kernel(
    back, nx, ny, xr, *refs
):
    if back:
        (inc_ref, slope_ref, w_hbm, mix_ref, bz_ref, bzs_ref, ky_ref, kyt_ref, bx_ref, bxr_ref,
         out_ref, modes_ref, got_ref, *scratch) = refs
    else:
        (inc_ref, w_hbm, mix_ref, bias_ref, bz_ref, bzs_ref, ky_ref, kyt_ref, bx_ref, bxr_ref,
         out_ref, modes_ref, got_ref, *scratch) = refs
    (w_ref, sig_ref, ghi_ref, glo_ref, s_ref, r_ref, m_ref, p_ref, q_ref, qs_ref,
     send1, recv1, send2, recv2, wsem) = scratch
    channels, _, yr, zr = inc_ref.shape
    cl, jl, xp = MODES // nx, MODES // ny, r_ref.shape[2]
    n = nx * ny
    lanes = jl * channels
    gx, gy = lax.axis_index("gx"), lax.axis_index("gy")
    me = gx * ny + gy

    wcopy = pltpu.make_async_copy(w_hbm, w_ref, wsem)
    wcopy.start()

    barrier = pltpu.get_barrier_semaphore()

    def greet(k, carry):
        peer = lax.rem(me + k, n)
        pl.semaphore_signal(
            barrier, inc=1,
            device_id={"gx": peer // ny, "gy": lax.rem(peer, ny)},
            device_id_type=pl.DeviceIdType.MESH,
        )
        return carry

    lax.fori_loop(1, n, greet, 0)

    def along_z(x, carry):
        if back:
            signal = inc_ref[:, x].astype(f32) * slope_ref[:, x]
            sig_ref[:, x] = signal
            block = signal.astype(bf16)
        else:
            block = inc_ref[:, x]
        block = block.reshape(channels * yr, zr)
        g = dot(bz_ref[0], block, 1, 1) + dot(bz_ref[1], block, 1, 1)
        ghi, glo = split(g)
        rows = pl.ds(pl.multiple_of(x * MODES, MODES), MODES)
        ghi_ref[rows, :] = ghi
        glo_ref[rows, :] = glo
        return carry

    lax.fori_loop(0, xr, along_z, 0)
    ghi = ghi_ref[...]
    t = dot(ghi, ky_ref[0]) + dot(ghi, ky_ref[1]) + dot(glo_ref[...], ky_ref[0])
    t = jnp.swapaxes(t.reshape(xr, MODES, ny * lanes), 0, 1)
    if xp > xr:
        t = jnp.concatenate([t, jnp.zeros((MODES, xp - xr, ny * lanes), f32)], axis=1)
    t = t.astype(bf16)
    for h in range(ny):
        s_ref[h] = t[:, :, h * lanes : (h + 1) * lanes].reshape(nx, cl, xp, lanes)

    pl.semaphore_wait(barrier, n - 1)

    def exchange(source, target, send, recv):
        def copy_to(peer, slot_of):
            return pltpu.make_async_remote_copy(
                src_ref=source(peer // ny, lax.rem(peer, ny)),
                dst_ref=target.at[lax.rem(slot_of, ny) * nx + slot_of // ny],
                send_sem=send.at[peer],
                recv_sem=recv.at[slot_of],
                device_id={"gx": peer // ny, "gy": lax.rem(peer, ny)},
                device_id_type=pl.DeviceIdType.MESH,
            )

        def begin(k, carry):
            copy_to(lax.rem(me + k, n), me).start()
            return carry

        def finish(k, carry):
            copy_to(lax.rem(me + k, n), me).wait_send()
            peer = lax.rem(me + n - k, n)
            copy_to(peer, peer).wait_recv()
            return carry

        lax.fori_loop(1, n, begin, 0)
        target[gy * nx + gx] = source(gx, gy)[...]
        lax.fori_loop(1, n, finish, 0)

    exchange(lambda d, h: s_ref.at[h, d], r_ref, send1, recv1)

    for c in range(cl):
        part = r_ref[:, c].reshape(n * xp, lanes)
        own = dot(bx_ref[0], part) + dot(bx_ref[1], part)
        modes_ref[c] = own.T.reshape(jl, channels, MODES)
    wcopy.wait()

    def mix(j, carry):
        for c in range(cl):
            own = modes_ref[c, j]
            weight = w_ref[j, c]
            if back:
                m_ref[c, j] = jnp.sum(weight * own[None], axis=1)
            else:
                m_ref[c, j] = jnp.sum(weight * own[:, None, :], axis=0)
        return carry

    lax.fori_loop(0, jl, mix, 0)
    for c in range(cl):
        top, rest = split(m_ref[c].reshape(lanes, MODES))
        spread = (
            dot(bxr_ref[0], top, 1, 1) + dot(bxr_ref[1], top, 1, 1) + dot(bxr_ref[0], rest, 1, 1)
        )
        p_ref[:, c] = spread.astype(bf16).reshape(nx, xp, lanes)

    exchange(lambda d, h: p_ref.at[d], q_ref, send2, recv2)

    got = [q_ref[h * nx : (h + 1) * nx].reshape(MODES, xp, lanes) for h in range(ny)]
    got = jnp.concatenate(got, axis=2).astype(f32)
    got = jnp.swapaxes(got, 0, 1)[:xr].reshape(xr * MODES, ny * lanes).astype(bf16)
    got_ref[...] = got
    qs_ref[...] = dot(got, kyt_ref[0]) + dot(got, kyt_ref[1])

    def finish_field(x, carry):
        rows = pl.ds(pl.multiple_of(x * MODES, MODES), MODES)
        top, rest = split(qs_ref[rows, :])
        stack = jnp.concatenate([top, rest, top], axis=0)
        field = dot(stack, bzs_ref[...], 0, 0).reshape(channels, yr, zr)
        if back:
            values = [sig_ref[i, x] for i in range(channels)]
        else:
            values = [inc_ref[i, x].astype(f32) for i in range(channels)]
        for o in range(channels):
            total = field[o]
            for i in range(channels):
                total = total + (mix_ref[i, o] if back else mix_ref[o, i]) * values[i]
            if back:
                out_ref[o, x] = total.astype(bf16)
            else:
                total = total + bias_ref[0, o]
                cdf = 0.5 * (1.0 + lax.erf(total * 0.7071067811865476))
                out_ref[o, x] = cdf + total * jnp.exp(-0.5 * total * total) * 0.3989422804014327
        return carry

    lax.fori_loop(0, xr, finish_field, 0)


def ahead_kernel(
    act_ref, cot_ref, got_ref, got_back_ref, mix_ref, bias_ref, bzs_ref, kyt_ref, out_ref,
    pre_ref, back_ref,
):
    channels, xr, yr, zr = act_ref.shape
    pre_ref[...] = dot(got_ref[...], kyt_ref[0]) + dot(got_ref[...], kyt_ref[1])
    back_ref[...] = dot(got_back_ref[...], kyt_ref[0]) + dot(got_back_ref[...], kyt_ref[1])

    def field_of(ref, x):
        rows = pl.ds(pl.multiple_of(x * MODES, MODES), MODES)
        top, rest = split(ref[rows, :])
        stack = jnp.concatenate([top, rest, top], axis=0)
        return dot(stack, bzs_ref[...], 0, 0).reshape(channels, yr, zr)

    def step(x, carry):
        field = field_of(pre_ref, x)
        values = [act_ref[i, x].astype(f32) for i in range(channels)]
        signals = []
        for o in range(channels):
            total = field[o]
            for i in range(channels):
                total = total + mix_ref[o, i] * values[i]
            total = total + bias_ref[0, o]
            cdf = 0.5 * (1.0 + lax.erf(total * 0.7071067811865476))
            slope = cdf + total * jnp.exp(-0.5 * total * total) * 0.3989422804014327
            signals.append(cot_ref[o, x].astype(f32) * slope)
        field = field_of(back_ref, x)
        for o in range(channels):
            total = field[o]
            for i in range(channels):
                total = total + mix_ref[i, o] * signals[i]
            out_ref[o, x] = total.astype(bf16)
        return carry

    lax.fori_loop(0, xr, step, 0)


def ahead(activations, cotangent, got, got_back, mixing, bias, bzs, kyt):
    channels, xr, yr, zr = activations.shape
    vmem = pl.BlockSpec(memory_space=pltpu.VMEM)
    smem = pl.BlockSpec(memory_space=pltpu.SMEM)
    return pl.pallas_call(
        ahead_kernel,
        out_shape=jax.ShapeDtypeStruct(activations.shape, bf16),
        in_specs=[vmem] * 4 + [smem] * 2 + [vmem] * 2,
        out_specs=vmem,
        scratch_shapes=[pltpu.VMEM((xr * MODES, channels * yr), f32)] * 2,
        compiler_params=pltpu.CompilerParams(vmem_limit_bytes=50 * 2**20),
        cost_estimate=pl.CostEstimate(flops=10**9, bytes_accessed=10**7, transcendentals=10**6),
    )(activations, cotangent, got, got_back, mixing, bias, bzs, kyt)


def block_turn(back, nx, ny, collective, field, slope, weights, mixing, bias, tables):
    channels, xr, yr, zr = field.shape
    xp = -(-xr // 16) * 16
    cl, jl, n = MODES // nx, MODES // ny, nx * ny
    lanes = jl * channels
    vmem = pl.BlockSpec(memory_space=pltpu.VMEM)
    smem = pl.BlockSpec(memory_space=pltpu.SMEM)
    hbm = pl.BlockSpec(memory_space=pl.ANY)
    if back:
        args = (field, slope, weights, mixing, *tables)
        specs = [vmem, vmem, hbm, smem] + [vmem] * len(tables)
    else:
        args = (field, weights, mixing, bias, *tables)
        specs = [vmem, hbm, smem, smem] + [vmem] * len(tables)
    dma = pltpu.SemaphoreType.DMA
    return pl.pallas_call(
        functools.partial(kernel, back, nx, ny, xr),
        out_shape=(
            jax.ShapeDtypeStruct(field.shape, bf16 if back else f32),
            jax.ShapeDtypeStruct((cl, jl, channels, MODES), f32),
            jax.ShapeDtypeStruct((xr * MODES, ny * lanes), bf16),
        ),
        in_specs=specs,
        out_specs=(vmem, vmem, vmem),
        scratch_shapes=[
            pltpu.VMEM(weights.shape, f32),
            pltpu.VMEM(field.shape if back else (8, 128), f32),
            pltpu.VMEM((xr * MODES, channels * yr), bf16),
            pltpu.VMEM((xr * MODES, channels * yr), bf16),
            pltpu.VMEM((ny, nx, cl, xp, lanes), bf16),
            pltpu.VMEM((n, cl, xp, lanes), bf16),
            pltpu.VMEM((cl, jl, channels, MODES), f32),
            pltpu.VMEM((nx, cl, xp, lanes), bf16),
            pltpu.VMEM((n, cl, xp, lanes), bf16),
            pltpu.VMEM((xr * MODES, channels * yr), f32),
            dma((n,)), dma((n,)), dma((n,)), dma((n,)), dma,
        ],
        compiler_params=pltpu.CompilerParams(
            collective_id=collective, has_side_effects=True, vmem_limit_bytes=50 * 2**20
        ),
        cost_estimate=pl.CostEstimate(flops=10**9, bytes_accessed=2 * 10**7, transcendentals=10**6),
    )(*args)


def body(activations, cotangent, spectral_weights, pointwise, channel_bias):
    inputs = activations[0]
    channels, xr, yr, zr = inputs.shape
    nx, ny = lax.axis_size("gx"), lax.axis_size("gy")
    xp = -(-xr // 16) * 16
    bz = trig_basis(zr)
    bx = trig_basis(xr * nx).reshape(MODES, nx, xr)
    bx = np.concatenate([bx, np.zeros((MODES, nx, xp - xr))], axis=2).reshape(MODES, nx * xp)
    by = trig_basis(yr * ny).reshape(MODES, ny, yr)
    kron = np.einsum("jgy,ik->giyjk", by, np.eye(channels)).reshape(
        ny, channels * yr, MODES * channels
    )
    bzh = halves(bz)
    kh = halves(kron)
    gy = lax.axis_index("gy")
    ky = lax.dynamic_index_in_dim(jnp.asarray(np.swapaxes(kh, 0, 1)), gy, 0, False)
    kyt = lax.dynamic_index_in_dim(
        jnp.asarray(np.ascontiguousarray(np.transpose(kh, (1, 0, 3, 2)))), gy, 0, False
    )
    tables = (
        jnp.asarray(bzh),
        jnp.asarray(np.concatenate([bzh[0], bzh[0], bzh[1]], axis=0)),
        ky,
        kyt,
        jnp.asarray(halves(np.concatenate([bx] * ny, axis=1))),
        jnp.asarray(halves(bx.T)),
    )
    weights = spectral_weights[0]
    mixing = pointwise[0]
    following = [from_behind(v, "segment", -1) for v in (inputs, mixing, channel_bias)]
    slope, input_modes, got = block_turn(
        False, nx, ny, 0, inputs, None, weights, mixing, channel_bias, tables
    )
    next_got = from_behind(got, "segment", -1)
    segment_index = lax.axis_index("segment")
    segment_count = lax.axis_size("segment")
    incoming = cotangent
    kept_grad = jnp.zeros(cotangent.shape, bf16)
    kept_modes = jnp.zeros(input_modes.shape, f32)
    for turn_index in range(segment_count):
        active = segment_index == segment_count - 1 - turn_index
        input_grad, grad_modes, got_back = block_turn(
            True, nx, ny, 1 + turn_index, incoming, slope, weights, mixing, None, tables
        )
        kept_grad = jnp.where(active, input_grad, kept_grad)
        kept_modes = jnp.where(active, grad_modes, kept_modes)
        if turn_index == 0 and segment_count > 1:
            next_back = from_behind(got_back, "segment", -1)
            incoming = ahead(
                following[0], cotangent, next_got, next_back, following[1], following[2],
                tables[1], tables[3],
            )
        elif turn_index + 1 < segment_count:
            incoming = from_behind(input_grad, "segment", -1)
    input_modes = jnp.swapaxes(input_modes, 0, 1)
    kept_modes = jnp.swapaxes(kept_modes, 0, 1)
    weight_grad = input_modes[:, :, :, None, :] * kept_modes[:, :, None, :, :]
    return (kept_grad[None], weight_grad[None])


def solution(mesh):
    return jax.shard_map(
        body,
        mesh=mesh,
        in_specs=(
            P("segment", "groups", "gx", "gy", None),
            P("groups", "gx", "gy", None),
            P("segment", "gy", "gx", None, None, None),
            P("segment", None, None),
            P("segment", None),
        ),
        out_specs=(
            P("segment", "groups", "gx", "gy", None),
            P("segment", "gy", "gx", "groups", None, None),
        ),
        check_vma=False,
    )
```

profile of v0, /device:TPU:0, one launch (start us, length us, event | category | flops | bytes accessed | tf_op | source)
XLA Modules:
  0.0 136.4 jit_solution(1645224405200824689)
XLA Ops:
  0.6 0.0 copy-start.4
  0.6 0.0 copy-start.1
  0.7 0.0 copy-start.11
  0.7 1.4 %collective-permute-start = (bf16[8,16,64,128]{3,2,1,0:T(8,128)(2,1)}, bf16[8,16,64,128]{3,2,1,0:T(8,128)(2,1)}, u32[]{:S(2)}, u32[]{:S(2)}) collective-permute-start(bf16[8,16,64,128]{3,2,1,0:T(8,128)(2,1)} %bitcast.15), channel_id=1, source_target_pairs={{1,0},{3,2},{5,4},{7,6},{9,8},{11,10},{13,12},{15,14},{17,16},{19,... | collective-permute-start | bytes 6291464 | tf_op jit(solution)/shard_map/ppermute | solution.py:20
  2.1 1.1 dynamic-slice_bitcast_fusion.refs_7_.kyt_ref
  3.2 1.1 dynamic-slice_bitcast_fusion.1.refs_6_
  4.3 0.0 copy-done.4
  4.3 0.0 copy-done.1
  4.3 0.0 copy-done.11
  4.3 0.0 copy-start.2
  4.3 0.8 copy-done.2
  5.1 0.0 copy-start.5
  5.1 0.8 copy-done.5
  5.9 0.0 copy-start.9
  5.9 0.7 copy-done.9
  6.6 0.0 copy-start.3
  6.6 31.8 %shard_map.122 = (f32[8,16,64,128]{3,2,1,0:T(8,128)}, f32[4,16,8,32]{3,2,1,0:T(8,128)S(1)}, bf16[512,256]{1,0:T(8,128)(2,1)}) custom-call(bf16[8,16,64,128]{3,2,1,0:T(8,128)(2,1)S(1)} %bitcast.16, f32[16,4,8,8,32]{4,3,2,1,0:T(8,128)} %bitcast.17, f32[8,8]{1,0:T(8,128)} %bitcast.2.refs_2_.refs_3_, f32[1,8]{1,0:T(1,128)S(1)} %copy-done.11, ...), custom_call_target="tpu_custom_call" | custom-call | flops 1000000000 | bytes 20000000 | tf_op jit(solution)/shard_map/pallas_call | solution.py:262
  38.4 0.0 copy-done.3
  38.4 31.6 %shard_map.123 = (bf16[8,16,64,128]{3,2,1,0:T(8,128)(2,1)S(1)}, f32[4,16,8,32]{3,2,1,0:T(8,128)S(1)}, bf16[512,256]{1,0:T(8,128)(2,1)}) custom-call(bf16[8,16,64,128]{3,2,1,0:T(8,128)(2,1)} %cot_ref.1, f32[8,16,64,128]{3,2,1,0:T(8,128)} %get-tuple-element.11.refs_1_, f32[16,4,8,8,32]{4,3,2,1,0:T(8,128)} %bitcast.18, f32[8,8]{1,0:T(8,128)} %bitcast.2.refs_2_.refs_3_, ...), custom_call_target="tpu_custom_call" | custom-call | flops 1000000000 | bytes 20000000 | tf_op jit(solution)/shard_map/pallas_call | solution.py:262
  70.0 0.0 copy-start.7
  70.0 0.7 copy-done.7
  70.7 1.3 collective-permute-start.2
  72.0 1.3 collective-permute-start.1
  73.3 1.3 collective-permute-start.3
  74.6 1.3 collective-permute-start.4
  75.9 0.0 copy-start.6
  75.9 0.0 copy-start.10
  75.9 12.4 %collective-permute-done.4.bias_ref = f32[1,8]{1,0:T(1,128)S(1)} collective-permute-done((f32[1,8]{1,0:T(1,128)S(1)}, f32[1,8]{1,0:T(1,128)S(1)}, u32[]{:S(2)}, u32[]{:S(2)}) %collective-permute-start.4) | collective-permute-done | bytes 64 | tf_op jit(solution)/shard_map/ppermute | solution.py:20
  88.3 0.0 collective-permute-done.3.mix_ref
  88.3 0.0 collective-permute-done.2.got_back_ref
  88.3 0.0 collective-permute-done.1.got_ref
  88.3 0.0 collective-permute-done.act_ref
  88.3 12.9 %shard_map.124.refs_0_ = bf16[8,16,64,128]{3,2,1,0:T(8,128)(2,1)S(1)} custom-call(bf16[8,16,64,128]{3,2,1,0:T(8,128)(2,1)} %collective-permute-done.act_ref, bf16[8,16,64,128]{3,2,1,0:T(8,128)(2,1)} %cot_ref.1, bf16[512,256]{1,0:T(8,128)(2,1)} %collective-permute-done.1.got_ref, bf16[512,256]{1,0:T(8,128)(2,1)} %collective-permute-done.2.got_back_ref, ...), custom_call_target="tpu_custom_call" | custom-call | flops 1000000000 | bytes 10000000 | tf_op jit(solution)/shard_map/pallas_call | solution.py:236
  101.2 0.0 copy-start
  101.3 1.3 copy-done
  102.6 0.0 copy-done.6
  102.6 0.0 copy-done.10
  102.6 0.0 copy-start.8
  102.6 30.5 %shard_map.125 = (bf16[8,16,64,128]{3,2,1,0:T(8,128)(2,1)S(1)}, f32[4,16,8,32]{3,2,1,0:T(8,128)S(1)}, bf16[512,256]{1,0:T(8,128)(2,1)}) custom-call(bf16[8,16,64,128]{3,2,1,0:T(8,128)(2,1)} %copy-done, f32[8,16,64,128]{3,2,1,0:T(8,128)} %get-tuple-element.11.refs_1_, f32[16,4,8,8,32]{4,3,2,1,0:T(8,128)} %bitcast.19, f32[8,8]{1,0:T(8,128)} %bitcast.2.refs_2_.refs_3_, ...), custom_call_target="tpu_custom_call" | custom-call | flops 1000000000 | bytes 20000000 | tf_op jit(solution)/shard_map/pallas_call | solution.py:262
  133.1 0.0 copy-done.8
  133.2 1.7 %broadcast_multiply_fusion = f32[1,16,4,8,8,32]{5,4,3,2,1,0:T(8,128)} fusion(f32[4,16,8,32]{3,2,1,0:T(8,128)S(1)} %get-tuple-element.15, f32[16,4,8,32]{3,2,0,1:T(8,128)S(1)} %select_bitcast_fusion.1), kind=kLoop, calls=%fused_computation.1 | loop fusion | flops 131072 | bytes 655360 | tf_op jit(solution)/shard_map/mul | solution.py:347
  134.8 1.5 %select_bitcast_fusion = bf16[1,8,16,64,128]{4,3,2,1,0:T(8,128)(2,1)} fusion(bf16[8,16,64,128]{3,2,1,0:T(8,128)(2,1)S(1)} %get-tuple-element.13, bf16[8,16,64,128]{3,2,1,0:T(8,128)(2,1)S(1)} %get-tuple-element.14, pred[]{:T(512)S(6)} %eq.7, pred[]{:T(512)S(6)} %eq.6), kind=kLoop, calls=%fused_computation | loop fusion | flops 2097152 | bytes 6291458 | tf_op jit(solution)/shard_map/broadcast_in_dim | solution.py:348
  (1 shorter events, 0.0 us)
Async XLA Ops:
  0.6 3.6 %copy-start.4 = (bf16[96,128]{1,0:T(8,128)(2,1)S(1)}, bf16[96,128]{1,0:T(8,128)(2,1)}, u32[]{:S(2)}) copy-start(bf16[96,128]{1,0:T(8,128)(2,1)} %constant.38.clone.refs_5_.bzs_ref) | copy-start | bytes 73732
  0.6 3.6 %copy-start.1 = (bf16[1,8,16,64,128]{4,3,2,1,0:T(8,128)(2,1)S(1)}, bf16[1,8,16,64,128]{4,3,2,1,0:T(8,128)(2,1)}, u32[]{:S(2)}) copy-start(bf16[1,8,16,64,128]{4,3,2,1,0:T(8,128)(2,1)} %param.11) | copy-start | bytes 6291460
  0.7 3.6 %copy-start.11 = (f32[1,8]{1,0:T(1,128)S(1)}, f32[1,8]{1,0:T(1,128)}, u32[]{:S(2)}) copy-start(f32[1,8]{1,0:T(1,128)} %refs_3_.1) | copy-start | bytes 100
  0.7 87.7 %collective-permute-start = (bf16[8,16,64,128]{3,2,1,0:T(8,128)(2,1)}, bf16[8,16,64,128]{3,2,1,0:T(8,128)(2,1)}, u32[]{:S(2)}, u32[]{:S(2)}) collective-permute-start(bf16[8,16,64,128]{3,2,1,0:T(8,128)(2,1)} %bitcast.15), channel_id=1, source_target_pairs={{1,0},{3,2},{5,4},{7,6},{9,8},{11,10},{13,12},{15,14},{17,16},{19,... | collective-permute-start | bytes 6291464 | tf_op jit(solution)/shard_map/ppermute | solution.py:20
  4.3 0.8 copy-start.2
  5.1 0.8 copy-start.5
  5.9 0.7 copy-start.9
  6.6 31.8 %copy-start.3 = (bf16[2,128,32]{2,1,0:T(8,128)(2,1)S(1)}, bf16[2,128,32]{2,1,0:T(8,128)(2,1)}, u32[]{:S(2)}) copy-start(bf16[2,128,32]{2,1,0:T(8,128)(2,1)} %constant.40.clone.refs_9_) | copy-start | bytes 49156
  70.0 0.7 copy-start.7
  70.7 17.6 %collective-permute-start.2 = (bf16[512,256]{1,0:T(8,128)(2,1)}, bf16[512,256]{1,0:T(8,128)(2,1)}, u32[]{:S(2)}, u32[]{:S(2)}) collective-permute-start(bf16[512,256]{1,0:T(8,128)(2,1)} %get-tuple-element.12), channel_id=1, source_target_pairs={{1,0},{3,2},{5,4},{7,6},{9,8},{11,10},{13,12},{15,14},{17,16},{19,... | collective-permute-start | bytes 786440 | tf_op jit(solution)/shard_map/ppermute | solution.py:20
  72.0 16.3 %collective-permute-start.1 = (bf16[512,256]{1,0:T(8,128)(2,1)}, bf16[512,256]{1,0:T(8,128)(2,1)}, u32[]{:S(2)}, u32[]{:S(2)}) collective-permute-start(bf16[512,256]{1,0:T(8,128)(2,1)} %get-tuple-element.10), channel_id=1, source_target_pairs={{1,0},{3,2},{5,4},{7,6},{9,8},{11,10},{13,12},{15,14},{17,16},{19,... | collective-permute-start | bytes 786440 | tf_op jit(solution)/shard_map/ppermute | solution.py:20
  73.3 15.0 %collective-permute-start.3 = (f32[8,8]{1,0:T(8,128)}, f32[8,8]{1,0:T(8,128)S(1)}, u32[]{:S(2)}, u32[]{:S(2)}) collective-permute-start(f32[8,8]{1,0:T(8,128)} %bitcast.2.refs_2_.refs_3_), channel_id=1, source_target_pairs={{1,0},{3,2},{5,4},{7,6},{9,8},{11,10},{13,12},{15,14},{17,16},{19,... | collective-permute-start | bytes 776 | tf_op jit(solution)/shard_map/ppermute | solution.py:20
  74.6 13.7 %collective-permute-start.4 = (f32[1,8]{1,0:T(1,128)S(1)}, f32[1,8]{1,0:T(1,128)S(1)}, u32[]{:S(2)}, u32[]{:S(2)}) collective-permute-start(f32[1,8]{1,0:T(1,128)S(1)} %copy-done.11), channel_id=1, source_target_pairs={{1,0},{3,2},{5,4},{7,6},{9,8},{11,10},{13,12},{15,14},{17,16},{19,... | collective-permute-start | bytes 104 | tf_op jit(solution)/shard_map/ppermute | solution.py:20
  75.9 26.7 %copy-start.6 = (bf16[2,32,256]{2,1,0:T(8,128)(2,1)S(1)}, bf16[2,32,256]{2,1,0:T(8,128)(2,1)}, u32[]{:S(2)}) copy-start(bf16[2,32,256]{2,1,0:T(8,128)(2,1)} %constant.39.clone.refs_8_) | copy-start | bytes 98308
  75.9 26.7 %copy-start.10 = (bf16[2,32,128]{2,1,0:T(8,128)(2,1)S(1)}, bf16[2,32,128]{2,1,0:T(8,128)(2,1)}, u32[]{:S(2)}) copy-start(bf16[2,32,128]{2,1,0:T(8,128)(2,1)} %constant.37.clone.refs_4_) | copy-start | bytes 49156
  101.2 1.3 copy-start
  102.6 30.5 %copy-start.8 = (f32[4,16,8,32]{3,2,1,0:T(8,128)S(1)}, f32[4,16,8,32]{3,2,1,0:T(8,128)}, u32[]{:S(2)}) copy-start(f32[4,16,8,32]{3,2,1,0:T(8,128)} %copy-done.7) | copy-start | bytes 196612
where the time goes:
time: 137 us; the launch traced here: 136 us
  Pallas kernels  107 us (78%)
  waiting for transfers between devices  12.4 us (9%)
  starting transfers between devices  6.58 us (5%)
  local copies, waits for them, and re-layouts  6.52 us (5%)
  other arithmetic  3.23 us (2%)
    pallas_call x3, Pallas kernels, block_turn(): pl.pallas_call(functools.partial(kernel, back, nx, ny, xr), out_shape=(ja...  93.9 us
    pallas_call x1, Pallas kernels, ahead(): pl.pallas_call(ahead_kernel, out_shape=jax.ShapeDtypeStruct(activations.s...  12.9 us
    ppermute x5, waiting for transfers between devices, from_behind(): return lax.ppermute(block, axis, route)  12.4 us
    ppermute x5, starting transfers between devices, from_behind(): return lax.ppermute(block, axis, route)  6.58 us
    unnamed x24, local copies, waits for them, and re-layouts  4.36 us
  transfers between devices with their start and end apart: 5, of which 1 were waited for; matrix products, arithmetic and copies ran while one was open for 2% of the time, Pallas kernels for 46%

commit v1 on v0

--- a/solution.py
+++ b/solution.py
@@ -348,9 +348,456 @@
     return (kept_grad[None], weight_grad[None])
 
 
+def slope_of(value):
+    cdf = 0.5 * (1.0 + lax.erf(value * 0.7071067811865476))
+    return cdf + value * jnp.exp(-0.5 * value * value) * 0.3989422804014327
+
+
+def relay_kernel(
+    nx, ny, xq,
+    act_hbm, cot_hbm, w_hbm, mix_ref, bias_ref, mixv_ref, biasv_ref,
+    kyt_hbm, ky_hbm, bzf_hbm, bzi_hbm, bx_hbm, sp_hbm,
+    grad_hbm, wgrad_hbm,
+    act, act1, cot, w, wd, kyt, ky, bzf, bzi, bx, sp,
+    u, v, slope, sig, out, wgrad, in_modes, grad_modes, m_ref, mt_send, mt_recv,
+    mixv1, biasv1, mix1, bias1, s_ref, p_ref, r_ref,
+    load_sem, send_sem, recv_sem, row_send, row_recv, small_send, small_recv, store_sem,
+):
+    channels, xr, yr, zr = act.shape
+    n = nx * ny
+    cl, jl = MODES // nx, MODES // ny
+    nh, hq = r_ref.shape[1], r_ref.shape[3]
+    lanes = jl * channels
+    rows = channels * yr
+    gx, gy, seg = lax.axis_index("gx"), lax.axis_index("gy"), lax.axis_index("segment")
+    me = gx * ny + gy
+    mine = gy * nx + gx
+    first, last = seg == 0, seg == 1
+    mesh_ids = pl.DeviceIdType.MESH
+
+    loads = [
+        pltpu.make_async_copy(source, target, load_sem.at[k])
+        for k, (source, target) in enumerate(
+            [
+                (act_hbm, act), (bzf_hbm, bzf), (kyt_hbm.at[gy], kyt), (w_hbm, w), (bx_hbm, bx),
+                (sp_hbm, sp), (ky_hbm.at[gy], ky), (bzi_hbm, bzi), (cot_hbm, cot),
+            ]
+        )
+    ]
+    for load in loads:
+        load.start()
+
+    barrier = pltpu.get_barrier_semaphore()
+
+    def greet(k, carry):
+        peer = lax.rem(me + k, n)
+        pl.semaphore_signal(
+            barrier, inc=1,
+            device_id={"gx": peer // ny, "gy": lax.rem(peer, ny)},
+            device_id_type=mesh_ids,
+        )
+        return carry
+
+    lax.fori_loop(1, n, greet, 0)
+    pl.semaphore_signal(
+        barrier, inc=1, device_id={"segment": 1 - seg}, device_id_type=mesh_ids
+    )
+
+    def ahead(source, target, send, recv):
+        return pltpu.make_async_remote_copy(
+            src_ref=source, dst_ref=target, send_sem=send, recv_sem=recv,
+            device_id={"segment": 1 - seg}, device_id_type=mesh_ids,
+        )
+
+    def rows_copy(q):
+        part = pl.ds(q * xq, xq)
+        return ahead(act_hbm.at[:, part], act1.at[:, part], row_send.at[q], row_recv.at[q])
+
+    def modes_copy(k):
+        return ahead(mt_send.at[k], mt_recv.at[k], small_send.at[k], small_recv.at[k])
+
+    small = [
+        ahead(mixv_ref, mixv1, small_send.at[2], small_recv.at[2]),
+        ahead(biasv_ref, biasv1, small_send.at[3], small_recv.at[3]),
+    ]
+
+    def send(source, e, half):
+        def begin(k, carry):
+            peer = lax.rem(me + k, n)
+            d, h = peer // ny, lax.rem(peer, ny)
+            pltpu.make_async_remote_copy(
+                src_ref=source(d, h), dst_ref=r_ref.at[e, half, mine],
+                send_sem=send_sem.at[e, half], recv_sem=recv_sem.at[e, half],
+                device_id={"gx": d, "gy": h}, device_id_type=mesh_ids,
+            ).start()
+            return carry
+
+        lax.fori_loop(1, n, begin, 0)
+        r_ref[e, half, mine] = source(gx, gy)[...]
+
+    def arrive(e, half):
+        block = r_ref.at[e, half, pl.ds(0, n - 1)]
+        pltpu.make_async_copy(block, block, recv_sem.at[e, half]).wait()
+
+    def sent(e):
+        for half in range(nh):
+            block = r_ref.at[e, half, pl.ds(0, n - 1)]
+            pltpu.make_async_copy(block, block, send_sem.at[e, half]).wait()
+
+    def to_modes(block, k, half, q):
+        g = dot(block, bzf[...])
+        g = g[:, : nx * 16] + g[:, nx * 16 :]
+        top, rest = split(g)
+        t = dot(kyt[0], top) + dot(kyt[1], top) + dot(kyt[0], rest)
+        t = t.T.astype(bf16)
+        for h in range(ny):
+            s_ref[k, half, h * nx : (h + 1) * nx, q] = t[:, h * lanes : (h + 1) * lanes].reshape(
+                nx, 16, lanes
+            )
+
+    def to_field(e, half, q):
+        block = jnp.concatenate(
+            [
+                r_ref[e, half, h * nx : (h + 1) * nx, q].reshape(nx * 16, lanes)
+                for h in range(ny)
+            ],
+            axis=1,
+        )
+        top, rest = split(dot(ky[0], block, 1, 1) + dot(ky[1], block, 1, 1))
+        return dot(jnp.concatenate([top, rest, top], axis=1), bzi[...])
+
+    def row(field, x):
+        return field[:, x * zr : (x + 1) * zr].reshape(channels, yr, zr)
+
+    def send_modes(k, e, half):
+        send(lambda d, h: s_ref.at[k, half, h * nx + d], e, half)
+
+    def own_modes(e):
+        block = r_ref[e].reshape(nh * n * hq * 16, lanes)
+        own = dot(bx[0], block) + dot(bx[1], block)
+        return own.T.reshape(jl, channels, cl * MODES)
+
+    def send_cells(mt, k, e):
+        top, rest = split(mt)
+        cells = dot(sp[0], top) + dot(sp[1], top) + dot(sp[0], rest)
+        p_ref[k] = cells.astype(bf16).reshape(nh, nx, hq, 16, lanes)
+        for half in range(nh):
+            send(lambda d, h: p_ref.at[k, half, d], e, half)
+
+    def mixed():
+        return m_ref[...].reshape(lanes, cl * MODES).T
+
+    def mix_back(e):
+        for half in range(nh):
+            arrive(e, half)
+        grad_modes[...] = own_modes(e)
+
+        def step(j, carry):
+            m_ref[j] = jnp.sum(wd[j] * grad_modes[j][None], axis=1)
+            return carry
+
+        lax.fori_loop(0, jl, step, 0)
+
+    def blend(mixing, values, o, back):
+        total = (mixing[0, o] if back else mixing[o, 0]) * values[0]
+        for i in range(1, channels):
+            total = total + (mixing[i, o] if back else mixing[o, i]) * values[i]
+        return total
+
+    for load in loads[:3]:
+        load.wait()
+    for half in range(nh):
+        def step(q, carry):
+            x = (half * hq + q) * xq
+            block = [act[:, x + k].reshape(rows, zr) for k in range(xq)]
+            to_modes(jnp.concatenate(block, axis=1), 0, half, q)
+            return carry
+
+        lax.fori_loop(0, hq, step, 0)
+        if half == 0:
+            pl.semaphore_wait(barrier, n)
+
+            @pl.when(last)
+            def _():
+                for copy in small:
+                    copy.start()
+                for q in range(xr // xq):
+                    rows_copy(q).start()
+
+        send_modes(0, 0, half)
+
+    for load in loads[3:]:
+        load.wait()
+
+    def dense(j, carry):
+        for i in range(channels):
+            wd[j, i] = jnp.concatenate([w[j, c, i] for c in range(cl)], axis=1)
+        return carry
+
+    lax.fori_loop(0, jl, dense, 0)
+
+    def pointwise(x, carry):
+        values = [act[i, x].astype(f32) for i in range(channels)]
+        for o in range(channels):
+            u[o, x] = blend(mix_ref, values, o, False) + bias_ref[0, o]
+        return carry
+
+    lax.fori_loop(0, xr, pointwise, 0)
+
+    for half in range(nh):
+        arrive(0, half)
+    in_modes[...] = own_modes(0)
+
+    def mix(j, carry):
+        own = in_modes[j]
+        m_ref[j] = jnp.sum(wd[j] * own[:, None, :], axis=0)
+        return carry
+
+    lax.fori_loop(0, jl, mix, 0)
+    mt_send[0] = mixed()
+
+    @pl.when(last)
+    def _():
+        modes_copy(0).start()
+
+    send_cells(mt_send[0], 0, 1)
+
+    @pl.when(last)
+    def _():
+        for half in range(nh):
+            arrive(1, half)
+
+            def step(q, carry):
+                field = to_field(1, half, q)
+                x0 = (half * hq + q) * xq
+                blocks = []
+                for k in range(xq):
+                    signal = cot[:, x0 + k].astype(f32) * slope_of(row(field, k) + u[:, x0 + k])
+                    sig[:, x0 + k] = signal
+                    blocks.append(signal.astype(bf16).reshape(rows, zr))
+                to_modes(jnp.concatenate(blocks, axis=1), 1, half, q)
+                return carry
+
+            lax.fori_loop(0, hq, step, 0)
+            send_modes(1, 2, half)
+        mix_back(2)
+        mt_send[1] = mixed()
+        modes_copy(1).start()
+        send_cells(mt_send[1], 1, 3)
+
+    @pl.when(first)
+    def _():
+        modes_copy(0).wait_recv()
+        send_cells(mt_recv[0], 1, 2)
+        for copy in small:
+            copy.wait_recv()
+        for k, (source, target) in enumerate([(mixv1, mix1), (biasv1, bias1)]):
+            copy = pltpu.make_async_copy(source, target, store_sem.at[k])
+            copy.start()
+            copy.wait()
+        for half in range(nh):
+            arrive(1, half)
+
+            def step(q, carry):
+                field = to_field(1, half, q)
+                x0 = (half * hq + q) * xq
+                for k in range(xq):
+                    slope[:, x0 + k] = slope_of(row(field, k) + u[:, x0 + k])
+                return carry
+
+            lax.fori_loop(0, hq, step, 0)
+
+        def ahead_quarter(half, q):
+            rows_copy(half * hq + q).wait_recv()
+            field = to_field(2, half, q)
+            x0 = (half * hq + q) * xq
+            for k in range(xq):
+                values = [act1[i, x0 + k].astype(f32) for i in range(channels)]
+                here = row(field, k)
+                signals = []
+                for o in range(channels):
+                    pre = here[o] + blend(mix1, values, o, False) + bias1[0, o]
+                    signals.append(cot[o, x0 + k].astype(f32) * slope_of(pre))
+                for i in range(channels):
+                    v[i, x0 + k] = blend(mix1, signals, i, True)
+
+        def back_quarter(half, q):
+            field = to_field(3, half, q)
+            x0 = (half * hq + q) * xq
+            blocks = []
+            for k in range(xq):
+                incoming = (row(field, k) + v[:, x0 + k]).astype(bf16).astype(f32)
+                signal = incoming * slope[:, x0 + k]
+                sig[:, x0 + k] = signal
+                blocks.append(signal.astype(bf16).reshape(rows, zr))
+            to_modes(jnp.concatenate(blocks, axis=1), 1, half, q)
+
+        for half in range(nh):
+            arrive(2, half)
+        quarters = [(half, q) for half in range(nh) for q in range(hq)]
+        for half, q in quarters[:-1]:
+            ahead_quarter(half, q)
+        modes_copy(1).wait_recv()
+        send_cells(mt_recv[1], 2, 3)
+        for half in range(nh):
+            arrive(3, half)
+        for half, q in quarters:
+            if (half, q) == quarters[-1]:
+                ahead_quarter(half, q)
+            back_quarter(half, q)
+            if q == hq - 1:
+                send_modes(1, 4, half)
+        mix_back(4)
+        send_cells(mixed(), 3, 5)
+
+    def pointwise_back(x, carry):
+        values = [sig[i, x] for i in range(channels)]
+        for o in range(channels):
+            u[o, x] = blend(mix_ref, values, o, True)
+        return carry
+
+    lax.fori_loop(0, xr, pointwise_back, 0)
+
+    def weight_grad(j, carry):
+        for c in range(cl):
+            part = slice(c * MODES, (c + 1) * MODES)
+            wgrad[j, c] = in_modes[j][:, None, part] * grad_modes[j][None, :, part]
+        return carry
+
+    lax.fori_loop(0, jl, weight_grad, 0)
+    stores = [pltpu.make_async_copy(wgrad, wgrad_hbm, store_sem.at[0])]
+    stores[0].start()
+    e = 3 + 2 * (1 - seg)
+    for half in range(nh):
+        arrive(e, half)
+
+        def step(q, carry):
+            field = to_field(e, half, q)
+            x0 = (half * hq + q) * xq
+            for k in range(xq):
+                out[:, x0 + k] = (row(field, k) + u[:, x0 + k]).astype(bf16)
+            return carry
+
+        lax.fori_loop(0, hq, step, 0)
+        part = pl.ds(half * hq * xq, hq * xq)
+        store = pltpu.make_async_copy(out.at[:, part], grad_hbm.at[:, part], store_sem.at[1 + half])
+        store.start()
+        stores.append(store)
+    for e in range(4):
+        sent(e)
+
+    @pl.when(first)
+    def _():
+        sent(4)
+        sent(5)
+
+    @pl.when(last)
+    def _():
+        for copy in small:
+            copy.wait_send()
+        for q in range(xr // xq):
+            rows_copy(q).wait_send()
+        for k in range(2):
+            modes_copy(k).wait_send()
+
+    for store in stores:
+        store.wait()
+
+
+def two_section_body(activations, cotangent, spectral_weights, pointwise, channel_bias):
+    inputs = activations[0]
+    channels, xr, yr, zr = inputs.shape
+    nx, ny = lax.axis_size("gx"), lax.axis_size("gy")
+    n = nx * ny
+    cl, jl = MODES // nx, MODES // ny
+    xq = 16 // cl
+    nh = 2
+    hq = xr // (nh * xq)
+    lanes, rows = jl * channels, channels * yr
+    bz = trig_basis(zr).reshape(nx, cl, zr)
+    eye_x, eye_c = np.eye(xq), np.eye(cl)
+    bzf = np.einsum("dcz,xX->xzdXc", bz, eye_x).reshape(xq * zr, nx * 16)
+    bzi = halves(bzf.reshape(xq, zr, nx * 16).transpose(2, 0, 1).reshape(nx * 16, xq * zr))
+    by = trig_basis(yr * ny).reshape(MODES, ny, yr)
+    ky = np.einsum("jgy,ik->giyjk", by, np.eye(channels)).reshape(ny, rows, ny * lanes)
+    ky = halves(ky)
+    bx = trig_basis(xr * nx).reshape(MODES, nx, nh, hq, xq)
+    sp = np.einsum("adtqx,cC->tdqxCca", bx, eye_c).reshape(nh * nx * hq * 16, cl * MODES)
+    bxf = np.broadcast_to(
+        sp.reshape(nh, 1, nx * hq * 16, cl * MODES), (nh, ny, nx * hq * 16, cl * MODES)
+    )
+    bxf = bxf.reshape(nh * n * hq * 16, cl * MODES).T
+    bzf = halves(bzf)
+    tables = [
+        np.ascontiguousarray(ky.transpose(1, 0, 3, 2)),
+        np.ascontiguousarray(ky.transpose(1, 0, 2, 3)),
+        np.concatenate([bzf[0], bzf[1]], axis=1),
+        np.concatenate([bzi[0], bzi[0], bzi[1]], axis=0),
+        halves(bxf),
+        halves(sp),
+    ]
+    weights, mixing = spectral_weights[0], pointwise[0]
+    vmem = pl.BlockSpec(memory_space=pltpu.VMEM)
+    smem = pl.BlockSpec(memory_space=pltpu.SMEM)
+    hbm = pl.BlockSpec(memory_space=pl.ANY)
+    dma = pltpu.SemaphoreType.DMA
+    grid = inputs.shape
+    scratch = [
+        pltpu.VMEM(grid, bf16), pltpu.VMEM(grid, bf16), pltpu.VMEM(grid, bf16),
+        pltpu.VMEM(weights.shape, f32),
+        pltpu.VMEM((jl, channels, channels, cl * MODES), f32),
+        pltpu.VMEM((2, ny * lanes, rows), bf16),
+        pltpu.VMEM((2, rows, ny * lanes), bf16),
+        pltpu.VMEM((xq * zr, 2 * nx * 16), bf16),
+        pltpu.VMEM((3 * nx * 16, xq * zr), bf16),
+        pltpu.VMEM((2, cl * MODES, nh * n * hq * 16), bf16),
+        pltpu.VMEM((2, nh * nx * hq * 16, cl * MODES), bf16),
+        pltpu.VMEM(grid, f32), pltpu.VMEM(grid, f32), pltpu.VMEM(grid, f32), pltpu.VMEM(grid, f32),
+        pltpu.VMEM(grid, bf16),
+        pltpu.VMEM(weights.shape, f32),
+        pltpu.VMEM((jl, channels, cl * MODES), f32),
+        pltpu.VMEM((jl, channels, cl * MODES), f32),
+        pltpu.VMEM((jl, channels, cl * MODES), f32),
+        pltpu.VMEM((2, cl * MODES, lanes), f32),
+        pltpu.VMEM((2, cl * MODES, lanes), f32),
+        pltpu.VMEM(mixing.shape, f32), pltpu.VMEM(channel_bias.shape, f32),
+        pltpu.SMEM(mixing.shape, f32), pltpu.SMEM(channel_bias.shape, f32),
+        pltpu.VMEM((2, nh, n, hq, 16, lanes), bf16),
+        pltpu.VMEM((4, nh, nx, hq, 16, lanes), bf16),
+        pltpu.VMEM((6, nh, n, hq, 16, lanes), bf16),
+        dma((9,)), dma((6, nh)), dma((6, nh)),
+        dma((xr // xq,)), dma((xr // xq,)), dma((4,)), dma((4,)), dma((1 + nh,)),
+    ]
+    input_grad, weight_grad = pl.pallas_call(
+        functools.partial(relay_kernel, nx, ny, xq),
+        out_shape=(
+            jax.ShapeDtypeStruct(grid, bf16),
+            jax.ShapeDtypeStruct(weights.shape, f32),
+        ),
+        in_specs=[hbm, hbm, hbm, smem, smem, vmem, vmem] + [hbm] * len(tables),
+        out_specs=(hbm, hbm),
+        scratch_shapes=scratch,
+        compiler_params=pltpu.CompilerParams(
+            collective_id=0, has_side_effects=True, vmem_limit_bytes=58 * 2**20
+        ),
+        cost_estimate=pl.CostEstimate(
+            flops=4 * 10**9, bytes_accessed=2 * 10**7, transcendentals=10**7
+        ),
+    )(
+        inputs, cotangent, weights, mixing, channel_bias, mixing, channel_bias,
+        *[jnp.asarray(table) for table in tables],
+    )
+    return (input_grad[None], weight_grad[None])
+
+
+def fits(mesh):
+    nx = mesh.shape["gx"]
+    return mesh.shape["segment"] == 2 and mesh.shape["gy"] == 2 and nx == 8
+
+
 def solution(mesh):
     return jax.shard_map(
-        body,
+        two_section_body if fits(mesh) else body,
         mesh=mesh,
         in_specs=(
             P("segment", "groups", "gx", "gy", None),

time: 137 us -> 107 us (0.78)
  waiting for transfers between devices: 12.4 us -> 0 us
  starting transfers between devices: 6.58 us -> 0 us
  Pallas kernels: 107 us -> 101 us
  other arithmetic: 3.23 us -> 0 us
  local copies, waits for them, and re-layouts: 6.52 us -> 4.55 us
    ppermute x5 -> x0, waiting for transfers between devices: 12.4 us -> none  [from_behind(): return lax.ppermute(block, axis, route)]
    ppermute x5 -> x0, starting transfers between devices: 6.58 us -> none  [from_behind(): return lax.ppermute(block, axis, route)]
    pallas_call x4 -> x1, Pallas kernels: 107 us -> 101 us  [two_section_body(): pl.pallas_call(functools.partial(relay_kernel, nx, ny, xq), out_shape=(ja...]
    squeeze x2 -> x0, local copies, waits for them, and re-layouts: 2.17 us -> none  [the longest x1 1.08 us: body(): lax.dynamic_index_in_dim(jnp.asarray(np.ascontiguousarray(np.transpose(kh...]
    mul x1 -> x0, other arithmetic: 1.66 us -> none  [body(): weight_grad = input_modes[:, :, :, None, :] * kept_modes[:, :, None, :, :]]
    broadcast_in_dim x1 -> x0, other arithmetic: 1.54 us -> none  [body(): return (kept_grad[None], weight_grad[None])]
    unnamed x24 -> x4, local copies, waits for them, and re-layouts: 4.36 us -> 4.55 us
  transfers between devices with their start and end apart: 5 -> 0, of which waited for: 1 -> 0; matrix products, arithmetic and copies ran while one was open for 2% -> 0% of each run, Pallas kernels for 46% -> 0%
where the time goes in v1:
time: 107 us
  Pallas kernels  101 us (94%)
  local copies, waits for them, and re-layouts  4.55 us (4%)
    pallas_call x1, Pallas kernels, two_section_body(): pl.pallas_call(functools.partial(relay_kernel, nx, ny, xq), out_shape=(ja...  101 us
    unnamed x4, local copies, waits for them, and re-layouts  4.55 us

profile of v1, /device:TPU:0, one launch (start us, length us, event | category | flops | bytes accessed | tf_op | source)
XLA Modules:
  0.0 106.5 jit_solution(8478065727499193321)
XLA Ops:
  0.6 101.3 %shard_map.122 = (bf16[8,16,64,128]{3,2,1,0:T(8,128)(2,1)}, f32[16,4,8,8,32]{4,3,2,1,0:T(8,128)}) custom-call(bf16[8,16,64,128]{3,2,1,0:T(8,128)(2,1)} %bitcast.7, bf16[8,16,64,128]{3,2,1,0:T(8,128)(2,1)} %cot_hbm.1, f32[16,4,8,8,32]{4,3,2,1,0:T(8,128)} %bitcast.8, f32[8,8]{1,0:T(8,128)} %bitcast.9, f32[1,8]{1,0:T(1,128)} %biasv_ref.1, f32[8,8]{1,0:T(8,128)} %bitcast.10, ...), custom_call_target="tpu_custom_call" | custom-call | flops 4000000000 | bytes 20000000 | tf_op jit(solution)/shard_map/pallas_call | solution.py:771
  102.0 0.0 copy-start
  102.0 3.2 %copy.15 = bf16[1,8,16,64,128]{4,3,2,1,0:T(8,128)(2,1)} copy(bf16[1,8,16,64,128]{4,3,2,1,0:T(8,128)(2,1)} %bitcast.6) | data formatting | bytes 4194304
  105.2 0.0 copy-done
  105.2 1.3 %copy.16 = f32[1,16,4,8,8,32]{5,4,3,2,1,0:T(8,128)} copy(f32[1,16,4,8,8,32]{5,4,3,2,1,0:T(8,128)S(1)} %bitcast.5) | data formatting | bytes 1048576
Async XLA Ops:
  102.0 3.2 %copy-start = (f32[16,4,8,8,32]{4,3,2,1,0:T(8,128)S(1)}, f32[16,4,8,8,32]{4,3,2,1,0:T(8,128)}, u32[]{:S(2)}) copy-start(f32[16,4,8,8,32]{4,3,2,1,0:T(8,128)} %get-tuple-element.5) | copy-start | bytes 1572868

commit v2 on v1

--- a/solution.py
+++ b/solution.py
@@ -353,13 +353,23 @@
     return cdf + value * jnp.exp(-0.5 * value * value) * 0.3989422804014327
 
 
+def field_of(cells, ny, ky, bzi):
+    blocks = []
+    for h in range(ny):
+        block = cells(h)
+        blocks.append(block.reshape(block.shape[0] * block.shape[1], block.shape[2]))
+    block = jnp.concatenate(blocks, axis=1)
+    top, rest = split(dot(ky[0], block, 1, 1) + dot(ky[1], block, 1, 1))
+    return dot(jnp.concatenate([top, rest, top], axis=1), bzi[...])
+
+
 def relay_kernel(
-    nx, ny, xq,
+    nx, ny, xq, cuts,
     act_hbm, cot_hbm, w_hbm, mix_ref, bias_ref, mixv_ref, biasv_ref,
     kyt_hbm, ky_hbm, bzf_hbm, bzi_hbm, bx_hbm, sp_hbm,
-    grad_hbm, wgrad_hbm,
-    act, act1, cot, w, wd, kyt, ky, bzf, bzi, bx, sp,
-    u, v, slope, sig, out, wgrad, in_modes, grad_modes, m_ref, mt_send, mt_recv,
+    out, rest_ref, cells_ref, wgrad, ky, bzi,
+    act, act1, cot, w, wd, kyt, bzf, bx, sp,
+    u, v, slope, sig, in_modes, grad_modes, m_ref, mt_send, mt_recv,
     mixv1, biasv1, mix1, bias1, s_ref, p_ref, r_ref,
     load_sem, send_sem, recv_sem, row_send, row_recv, small_send, small_recv, store_sem,
 ):
@@ -409,9 +419,14 @@
             device_id={"segment": 1 - seg}, device_id_type=mesh_ids,
         )
 
-    def rows_copy(q):
-        part = pl.ds(q * xq, xq)
-        return ahead(act_hbm.at[:, part], act1.at[:, part], row_send.at[q], row_recv.at[q])
+    def row_copy(x):
+        return ahead(act_hbm.at[:, x], act1.at[:, x], row_send.at[x], row_recv.at[x])
+
+    def send_rows(start, stop):
+        @pl.when(last)
+        def _():
+            for x in range(start, stop):
+                row_copy(x).start()
 
     def modes_copy(k):
         return ahead(mt_send.at[k], mt_recv.at[k], small_send.at[k], small_recv.at[k])
@@ -444,27 +459,21 @@
             block = r_ref.at[e, half, pl.ds(0, n - 1)]
             pltpu.make_async_copy(block, block, send_sem.at[e, half]).wait()
 
-    def to_modes(block, k, half, q):
-        g = dot(block, bzf[...])
-        g = g[:, : nx * 16] + g[:, nx * 16 :]
-        top, rest = split(g)
+    def to_modes(blocks, k, half):
+        parts = []
+        for block in blocks:
+            g = dot(block, bzf[...])
+            parts.append(g[:, : nx * 16] + g[:, nx * 16 :])
+        top, rest = split(jnp.concatenate(parts, axis=1))
         t = dot(kyt[0], top) + dot(kyt[1], top) + dot(kyt[0], rest)
         t = t.T.astype(bf16)
-        for h in range(ny):
-            s_ref[k, half, h * nx : (h + 1) * nx, q] = t[:, h * lanes : (h + 1) * lanes].reshape(
-                nx, 16, lanes
-            )
+        for q in range(hq):
+            for h in range(ny):
+                part = t[q * nx * 16 : (q + 1) * nx * 16, h * lanes : (h + 1) * lanes]
+                s_ref[k, half, h * nx : (h + 1) * nx, q] = part.reshape(nx, 16, lanes)
 
     def to_field(e, half, q):
-        block = jnp.concatenate(
-            [
-                r_ref[e, half, h * nx : (h + 1) * nx, q].reshape(nx * 16, lanes)
-                for h in range(ny)
-            ],
-            axis=1,
-        )
-        top, rest = split(dot(ky[0], block, 1, 1) + dot(ky[1], block, 1, 1))
-        return dot(jnp.concatenate([top, rest, top], axis=1), bzi[...])
+        return field_of(lambda h: r_ref[e, half, h * nx : (h + 1) * nx, q], ny, ky, bzi)
 
     def row(field, x):
         return field[:, x * zr : (x + 1) * zr].reshape(channels, yr, zr)
@@ -504,26 +513,23 @@
             total = total + (mixing[i, o] if back else mixing[o, i]) * values[i]
         return total
 
+    pl.semaphore_wait(barrier, n)
+
+    @pl.when(last)
+    def _():
+        for copy in small:
+            copy.start()
+
+    send_rows(0, cuts[0])
     for load in loads[:3]:
         load.wait()
     for half in range(nh):
-        def step(q, carry):
+        blocks = []
+        for q in range(hq):
             x = (half * hq + q) * xq
             block = [act[:, x + k].reshape(rows, zr) for k in range(xq)]
-            to_modes(jnp.concatenate(block, axis=1), 0, half, q)
-            return carry
-
-        lax.fori_loop(0, hq, step, 0)
-        if half == 0:
-            pl.semaphore_wait(barrier, n)
-
-            @pl.when(last)
-            def _():
-                for copy in small:
-                    copy.start()
-                for q in range(xr // xq):
-                    rows_copy(q).start()
-
+            blocks.append(jnp.concatenate(block, axis=1))
+        to_modes(blocks, 0, half)
         send_modes(0, 0, half)
 
     for load in loads[3:]:
@@ -560,6 +566,7 @@
     def _():
         modes_copy(0).start()
 
+    send_rows(cuts[0], cuts[1])
     send_cells(mt_send[0], 0, 1)
 
     @pl.when(last)
@@ -567,22 +574,23 @@
         for half in range(nh):
             arrive(1, half)
 
-            def step(q, carry):
+            blocks = []
+            for q in range(hq):
                 field = to_field(1, half, q)
                 x0 = (half * hq + q) * xq
-                blocks = []
+                block = []
                 for k in range(xq):
                     signal = cot[:, x0 + k].astype(f32) * slope_of(row(field, k) + u[:, x0 + k])
                     sig[:, x0 + k] = signal
-                    blocks.append(signal.astype(bf16).reshape(rows, zr))
-                to_modes(jnp.concatenate(blocks, axis=1), 1, half, q)
-                return carry
-
-            lax.fori_loop(0, hq, step, 0)
+                    block.append(signal.astype(bf16).reshape(rows, zr))
+                blocks.append(jnp.concatenate(block, axis=1))
+            to_modes(blocks, 1, half)
             send_modes(1, 2, half)
         mix_back(2)
         mt_send[1] = mixed()
         modes_copy(1).start()
+        for x in range(cuts[1], xr):
+            row_copy(x).start()
         send_cells(mt_send[1], 1, 3)
 
     @pl.when(first)
@@ -608,10 +616,10 @@
             lax.fori_loop(0, hq, step, 0)
 
         def ahead_quarter(half, q):
-            rows_copy(half * hq + q).wait_recv()
             field = to_field(2, half, q)
             x0 = (half * hq + q) * xq
             for k in range(xq):
+                row_copy(x0 + k).wait_recv()
                 values = [act1[i, x0 + k].astype(f32) for i in range(channels)]
                 here = row(field, k)
                 signals = []
@@ -621,32 +629,37 @@
                 for i in range(channels):
                     v[i, x0 + k] = blend(mix1, signals, i, True)
 
-        def back_quarter(half, q):
-            field = to_field(3, half, q)
-            x0 = (half * hq + q) * xq
+        def back_half(half):
             blocks = []
-            for k in range(xq):
-                incoming = (row(field, k) + v[:, x0 + k]).astype(bf16).astype(f32)
-                signal = incoming * slope[:, x0 + k]
-                sig[:, x0 + k] = signal
-                blocks.append(signal.astype(bf16).reshape(rows, zr))
-            to_modes(jnp.concatenate(blocks, axis=1), 1, half, q)
+            for q in range(hq):
+                field = to_field(3, half, q)
+                x0 = (half * hq + q) * xq
+                block = []
+                for k in range(xq):
+                    incoming = (row(field, k) + v[:, x0 + k]).astype(bf16).astype(f32)
+                    signal = incoming * slope[:, x0 + k]
+                    sig[:, x0 + k] = signal
+                    block.append(signal.astype(bf16).reshape(rows, zr))
+                blocks.append(jnp.concatenate(block, axis=1))
+            to_modes(blocks, 1, half)
+            send_modes(1, 4, half)
 
         for half in range(nh):
             arrive(2, half)
         quarters = [(half, q) for half in range(nh) for q in range(hq)]
-        for half, q in quarters[:-1]:
+        early = cuts[1] // xq
+        for half, q in quarters[:early]:
             ahead_quarter(half, q)
         modes_copy(1).wait_recv()
         send_cells(mt_recv[1], 2, 3)
-        for half in range(nh):
-            arrive(3, half)
-        for half, q in quarters:
-            if (half, q) == quarters[-1]:
-                ahead_quarter(half, q)
-            back_quarter(half, q)
-            if q == hq - 1:
-                send_modes(1, 4, half)
+        for half, q in quarters[early:]:
+            ahead_quarter(half, q)
+            if (half, q) == (nh - 1, 0):
+                for back in range(nh):
+                    arrive(3, back)
+                for back in range(nh - 1):
+                    back_half(back)
+        back_half(nh - 1)
         mix_back(4)
         send_cells(mixed(), 3, 5)
 
@@ -665,24 +678,18 @@
         return carry
 
     lax.fori_loop(0, jl, weight_grad, 0)
-    stores = [pltpu.make_async_copy(wgrad, wgrad_hbm, store_sem.at[0])]
-    stores[0].start()
     e = 3 + 2 * (1 - seg)
-    for half in range(nh):
+    for half in range(nh - 1):
         arrive(e, half)
-
-        def step(q, carry):
+        for q in range(hq):
             field = to_field(e, half, q)
             x0 = (half * hq + q) * xq
             for k in range(xq):
                 out[:, x0 + k] = (row(field, k) + u[:, x0 + k]).astype(bf16)
-            return carry
-
-        lax.fori_loop(0, hq, step, 0)
-        part = pl.ds(half * hq * xq, hq * xq)
-        store = pltpu.make_async_copy(out.at[:, part], grad_hbm.at[:, part], store_sem.at[1 + half])
-        store.start()
-        stores.append(store)
+    done = (nh - 1) * hq * xq
+    rest_ref[...] = u[:, done:]
+    arrive(e, nh - 1)
+    cells_ref[...] = r_ref[e, nh - 1]
     for e in range(4):
         sent(e)
 
@@ -695,11 +702,35 @@
     def _():
         for copy in small:
             copy.wait_send()
-        for q in range(xr // xq):
-            rows_copy(q).wait_send()
+        for x in range(xr):
+            row_copy(x).wait_send()
         for k in range(2):
             modes_copy(k).wait_send()
 
+
+def finish_kernel(
+    nx, ny, xq, done_ref, rest_ref, cells_ref, wgrad, ky, bzi, grad_hbm, wgrad_hbm, out, sem
+):
+    channels, done, yr, zr = done_ref.shape
+    hq = cells_ref.shape[1]
+    stores = [
+        pltpu.make_async_copy(wgrad, wgrad_hbm, sem.at[0]),
+        pltpu.make_async_copy(done_ref, grad_hbm.at[:, pl.ds(0, done)], sem.at[1]),
+    ]
+    for store in stores:
+        store.start()
+    for q in range(hq):
+        field = field_of(lambda h: cells_ref[h * nx : (h + 1) * nx, q], ny, ky, bzi)
+        for k in range(xq):
+            x = q * xq + k
+            here = field[:, k * zr : (k + 1) * zr].reshape(channels, yr, zr)
+            out[:, x] = (here + rest_ref[:, x]).astype(bf16)
+        part = pl.ds(q * xq, xq)
+        store = pltpu.make_async_copy(
+            out.at[:, part], grad_hbm.at[:, pl.ds(done + q * xq, xq)], sem.at[2 + q]
+        )
+        store.start()
+        stores.append(store)
     for store in stores:
         store.wait()
 
@@ -742,19 +773,17 @@
     hbm = pl.BlockSpec(memory_space=pl.ANY)
     dma = pltpu.SemaphoreType.DMA
     grid = inputs.shape
+    done = grid[:1] + ((nh - 1) * hq * xq,) + grid[2:]
+    left = grid[:1] + (hq * xq,) + grid[2:]
     scratch = [
         pltpu.VMEM(grid, bf16), pltpu.VMEM(grid, bf16), pltpu.VMEM(grid, bf16),
         pltpu.VMEM(weights.shape, f32),
         pltpu.VMEM((jl, channels, channels, cl * MODES), f32),
         pltpu.VMEM((2, ny * lanes, rows), bf16),
-        pltpu.VMEM((2, rows, ny * lanes), bf16),
         pltpu.VMEM((xq * zr, 2 * nx * 16), bf16),
-        pltpu.VMEM((3 * nx * 16, xq * zr), bf16),
         pltpu.VMEM((2, cl * MODES, nh * n * hq * 16), bf16),
         pltpu.VMEM((2, nh * nx * hq * 16, cl * MODES), bf16),
         pltpu.VMEM(grid, f32), pltpu.VMEM(grid, f32), pltpu.VMEM(grid, f32), pltpu.VMEM(grid, f32),
-        pltpu.VMEM(grid, bf16),
-        pltpu.VMEM(weights.shape, f32),
         pltpu.VMEM((jl, channels, cl * MODES), f32),
         pltpu.VMEM((jl, channels, cl * MODES), f32),
         pltpu.VMEM((jl, channels, cl * MODES), f32),
@@ -766,27 +795,43 @@
         pltpu.VMEM((4, nh, nx, hq, 16, lanes), bf16),
         pltpu.VMEM((6, nh, n, hq, 16, lanes), bf16),
         dma((9,)), dma((6, nh)), dma((6, nh)),
-        dma((xr // xq,)), dma((xr // xq,)), dma((4,)), dma((4,)), dma((1 + nh,)),
+        dma((xr,)), dma((xr,)), dma((4,)), dma((4,)), dma((2,)),
     ]
-    input_grad, weight_grad = pl.pallas_call(
-        functools.partial(relay_kernel, nx, ny, xq),
+    parts = pl.pallas_call(
+        functools.partial(relay_kernel, nx, ny, xq, (3, 9)),
         out_shape=(
-            jax.ShapeDtypeStruct(grid, bf16),
-            jax.ShapeDtypeStruct(weights.shape, f32),
+            jax.ShapeDtypeStruct(done, bf16),
+            jax.ShapeDtypeStruct(left, f32),
+            jax.ShapeDtypeStruct((n, hq, 16, lanes), bf16),
+            pltpu.VMEM(weights.shape, f32),
+            jax.ShapeDtypeStruct((2, rows, ny * lanes), bf16),
+            jax.ShapeDtypeStruct((3 * nx * 16, xq * zr), bf16),
         ),
         in_specs=[hbm, hbm, hbm, smem, smem, vmem, vmem] + [hbm] * len(tables),
-        out_specs=(hbm, hbm),
+        out_specs=[vmem] * 6,
         scratch_shapes=scratch,
         compiler_params=pltpu.CompilerParams(
-            collective_id=0, has_side_effects=True, vmem_limit_bytes=58 * 2**20
+            collective_id=0, has_side_effects=True, vmem_limit_bytes=46 * 2**20
         ),
         cost_estimate=pl.CostEstimate(
             flops=4 * 10**9, bytes_accessed=2 * 10**7, transcendentals=10**7
         ),
     )(
         inputs, cotangent, weights, mixing, channel_bias, mixing, channel_bias,
-        *[jnp.asarray(table) for table in tables],
+        *[pltpu.with_memory_space_constraint(jnp.asarray(table), pltpu.HBM) for table in tables],
     )
+    input_grad, weight_grad = pl.pallas_call(
+        functools.partial(finish_kernel, nx, ny, xq),
+        out_shape=(
+            jax.ShapeDtypeStruct(grid, bf16),
+            jax.ShapeDtypeStruct(weights.shape, f32),
+        ),
+        in_specs=[vmem] * 6,
+        out_specs=(hbm, hbm),
+        scratch_shapes=[pltpu.VMEM(left, bf16), dma((2 + hq,))],
+        compiler_params=pltpu.CompilerParams(vmem_limit_bytes=24 * 2**20),
+        cost_estimate=pl.CostEstimate(flops=10**9, bytes_accessed=10**7, transcendentals=0),
+    )(*parts)
     return (input_grad[None], weight_grad[None])
 
 

time: 107 us -> 78.7 us (0.74)
  Pallas kernels: 101 us -> 76.3 us
  local copies, waits for them, and re-layouts: 4.55 us -> 1.33 us
    pallas_call x1 -> x2, Pallas kernels: 101 us -> 76.3 us  [the longest x1 74.1 us: two_section_body(): pl.pallas_call(functools.partial(relay_kernel, nx, ny, xq, (3, 9)), out_s...]
    unnamed x4, local copies, waits for them, and re-layouts: 4.55 us -> 1.33 us
where the time goes in v2:
time: 78.7 us; the launch traced here: 78.5 us
  Pallas kernels  76.3 us (97%)
  local copies, waits for them, and re-layouts  1.33 us (2%)
  between operations  0.85 us (1%)
    pallas_call x1, Pallas kernels, two_section_body(): pl.pallas_call(functools.partial(relay_kernel, nx, ny, xq, (3, 9)), out_s...  74.1 us
    pallas_call x1, Pallas kernels, two_section_body(): pl.pallas_call(functools.partial(finish_kernel, nx, ny, xq), out_shape=(j...  2.16 us

profile of v2, /device:TPU:0, one launch (start us, length us, event | category | flops | bytes accessed | tf_op | source)
XLA Modules:
  0.0 78.5 jit_solution(13944209715987160637)
XLA Ops:
  0.6 0.0 copy-start
  0.6 0.7 copy-done
  1.3 0.0 copy-start.1
  1.3 0.7 copy-done.1
  2.0 74.1 %shard_map.122 = (bf16[8,8,64,128]{3,2,1,0:T(8,128)(2,1)S(1)}, f32[8,8,64,128]{3,2,1,0:T(8,128)S(1)}, bf16[16,2,16,128]{3,2,1,0:T(8,128)(2,1)S(1)}, f32[16,4,8,8...) custom-call(bf16[8,16,64,128]{3,2,1,0:T(8,128)(2,1)} %bitcast.7, ...), custom_call_target="tpu_custom_call" | custom-call | flops 4000000000 | bytes 20000000 | tf_op jit(solution)/shard_map/pallas_call | solution.py:800
  76.1 2.2 %shard_map.123 = (bf16[8,16,64,128]{3,2,1,0:T(8,128)(2,1)}, f32[16,4,8,8,32]{4,3,2,1,0:T(8,128)}) custom-call(bf16[8,8,64,128]{3,2,1,0:T(8,128)(2,1)S(1)} %get-tuple-element.10.done_ref, f32[8,8,64,128]{3,2,1,0:T(8,128)S(1)} %get-tuple-element.11.rest_ref, bf16[16,2,16,128]{3,2,1,0:T(8,128)(2,1)S(1)} %get-tuple-element.12.cells_ref, ...), custom_call_target="tpu_custom_call" | custom-call | flops 1000000000 | bytes 10000000 | tf_op jit(solution)/shard_map/pallas_call | solution.py:823
Async XLA Ops:
  0.6 0.7 copy-start
  1.3 0.7 copy-start.1

commit v3 on v2

--- a/solution.py
+++ b/solution.py
@@ -365,13 +365,14 @@
 
 def relay_kernel(
     nx, ny, xq, cuts,
-    act_hbm, cot_hbm, w_hbm, mix_ref, bias_ref, mixv_ref, biasv_ref,
+    act_hbm, cot_hbm, w_hbm, mix_ref, bias_ref, mix_hbm, bias_hbm,
     kyt_hbm, ky_hbm, bzf_hbm, bzi_hbm, bx_hbm, sp_hbm,
     out, rest_ref, cells_ref, wgrad, ky, bzi,
     act, act1, cot, w, wd, kyt, bzf, bx, sp,
     u, v, slope, sig, in_modes, grad_modes, m_ref, mt_send, mt_recv,
     mixv1, biasv1, mix1, bias1, s_ref, p_ref, r_ref,
     load_sem, send_sem, recv_sem, row_send, row_recv, small_send, small_recv, store_sem,
+    tail_send, tail_recv,
 ):
     channels, xr, yr, zr = act.shape
     n = nx * ny
@@ -379,6 +380,7 @@
     nh, hq = r_ref.shape[1], r_ref.shape[3]
     lanes = jl * channels
     rows = channels * yr
+    tail = xr - xq
     gx, gy, seg = lax.axis_index("gx"), lax.axis_index("gy"), lax.axis_index("segment")
     me = gx * ny + gy
     mine = gy * nx + gx
@@ -400,18 +402,16 @@
     barrier = pltpu.get_barrier_semaphore()
 
     def greet(k, carry):
-        peer = lax.rem(me + k, n)
+        other = lax.rem(seg * n + me + k, 2 * n)
+        peer = lax.rem(other, n)
         pl.semaphore_signal(
             barrier, inc=1,
-            device_id={"gx": peer // ny, "gy": lax.rem(peer, ny)},
+            device_id={"segment": other // n, "gx": peer // ny, "gy": lax.rem(peer, ny)},
             device_id_type=mesh_ids,
         )
         return carry
 
-    lax.fori_loop(1, n, greet, 0)
-    pl.semaphore_signal(
-        barrier, inc=1, device_id={"segment": 1 - seg}, device_id_type=mesh_ids
-    )
+    lax.fori_loop(1, 2 * n, greet, 0)
 
     def ahead(source, target, send, recv):
         return pltpu.make_async_remote_copy(
@@ -423,43 +423,63 @@
         return ahead(act_hbm.at[:, x], act1.at[:, x], row_send.at[x], row_recv.at[x])
 
     def send_rows(start, stop):
-        @pl.when(last)
-        def _():
-            for x in range(start, stop):
-                row_copy(x).start()
+        for x in range(start, stop):
+            row_copy(x).start()
 
     def modes_copy(k):
         return ahead(mt_send.at[k], mt_recv.at[k], small_send.at[k], small_recv.at[k])
 
     small = [
-        ahead(mixv_ref, mixv1, small_send.at[2], small_recv.at[2]),
-        ahead(biasv_ref, biasv1, small_send.at[3], small_recv.at[3]),
+        ahead(mix_hbm, mixv1, small_send.at[2], small_recv.at[2]),
+        ahead(bias_hbm, biasv1, small_send.at[3], small_recv.at[3]),
     ]
 
-    def send(source, e, half):
+    def send(source, target, sends, receives):
         def begin(k, carry):
             peer = lax.rem(me + k, n)
             d, h = peer // ny, lax.rem(peer, ny)
             pltpu.make_async_remote_copy(
-                src_ref=source(d, h), dst_ref=r_ref.at[e, half, mine],
-                send_sem=send_sem.at[e, half], recv_sem=recv_sem.at[e, half],
+                src_ref=source(d, h), dst_ref=target, send_sem=sends, recv_sem=receives,
                 device_id={"gx": d, "gy": h}, device_id_type=mesh_ids,
             ).start()
             return carry
 
         lax.fori_loop(1, n, begin, 0)
-        r_ref[e, half, mine] = source(gx, gy)[...]
+        target[...] = source(gx, gy)[...]
+
+    def send_half(source, e, half):
+        send(source, r_ref.at[e, half, mine], send_sem.at[e, half], recv_sem.at[e, half])
+
+    def send_quarter(source, e, half, q):
+        send(source, r_ref.at[e, half, mine, q], send_sem.at[e, half], recv_sem.at[e, half])
+
+    def send_tail(k, carry):
+        peer = lax.rem(me + k, n)
+        d, h = peer // ny, lax.rem(peer, ny)
+        pltpu.make_async_remote_copy(
+            src_ref=s_ref.at[2, nh - 1, h * nx + d, hq - 1],
+            dst_ref=r_ref.at[4, nh - 1, mine, hq - 1],
+            send_sem=tail_send.at[0], recv_sem=tail_recv.at[0],
+            device_id={"segment": 0, "gx": d, "gy": h}, device_id_type=mesh_ids,
+        ).start()
+        return carry
+
+    def await_block(block, sem):
+        pltpu.make_async_copy(block, block, sem).wait()
 
     def arrive(e, half):
-        block = r_ref.at[e, half, pl.ds(0, n - 1)]
-        pltpu.make_async_copy(block, block, recv_sem.at[e, half]).wait()
-
-    def sent(e):
-        for half in range(nh):
-            block = r_ref.at[e, half, pl.ds(0, n - 1)]
-            pltpu.make_async_copy(block, block, send_sem.at[e, half]).wait()
-
-    def to_modes(blocks, k, half):
+        await_block(r_ref.at[e, half, pl.ds(0, n - 1)], recv_sem.at[e, half])
+
+    def arrive_quarter(e, half, q):
+        await_block(r_ref.at[e, half, pl.ds(0, n - 1), q], recv_sem.at[e, half])
+
+    def sent(e, half):
+        await_block(r_ref.at[e, half, pl.ds(0, n - 1)], send_sem.at[e, half])
+
+    def sent_quarter(e, half, q):
+        await_block(r_ref.at[e, half, pl.ds(0, n - 1), q], send_sem.at[e, half])
+
+    def to_modes(blocks, k, half, q0):
         parts = []
         for block in blocks:
             g = dot(block, bzf[...])
@@ -467,10 +487,10 @@
         top, rest = split(jnp.concatenate(parts, axis=1))
         t = dot(kyt[0], top) + dot(kyt[1], top) + dot(kyt[0], rest)
         t = t.T.astype(bf16)
-        for q in range(hq):
+        for q in range(len(blocks)):
             for h in range(ny):
                 part = t[q * nx * 16 : (q + 1) * nx * 16, h * lanes : (h + 1) * lanes]
-                s_ref[k, half, h * nx : (h + 1) * nx, q] = part.reshape(nx, 16, lanes)
+                s_ref[k, half, h * nx : (h + 1) * nx, q0 + q] = part.reshape(nx, 16, lanes)
 
     def to_field(e, half, q):
         return field_of(lambda h: r_ref[e, half, h * nx : (h + 1) * nx, q], ny, ky, bzi)
@@ -479,26 +499,27 @@
         return field[:, x * zr : (x + 1) * zr].reshape(channels, yr, zr)
 
     def send_modes(k, e, half):
-        send(lambda d, h: s_ref.at[k, half, h * nx + d], e, half)
+        send_half(lambda d, h: s_ref.at[k, half, h * nx + d], e, half)
 
     def own_modes(e):
         block = r_ref[e].reshape(nh * n * hq * 16, lanes)
         own = dot(bx[0], block) + dot(bx[1], block)
         return own.T.reshape(jl, channels, cl * MODES)
 
+    def cells_of(table, mt):
+        top, rest = split(mt)
+        return (dot(table[0], top) + dot(table[1], top) + dot(table[0], rest)).astype(bf16)
+
     def send_cells(mt, k, e):
-        top, rest = split(mt)
-        cells = dot(sp[0], top) + dot(sp[1], top) + dot(sp[0], rest)
-        p_ref[k] = cells.astype(bf16).reshape(nh, nx, hq, 16, lanes)
+        table = [sp[i].reshape(nh * nx * hq * 16, cl * MODES) for i in range(2)]
+        p_ref[k] = cells_of(table, mt).reshape(nh, nx, hq, 16, lanes)
         for half in range(nh):
-            send(lambda d, h: p_ref.at[k, half, d], e, half)
+            send_half(lambda d, h: p_ref.at[k, half, d], e, half)
 
     def mixed():
         return m_ref[...].reshape(lanes, cl * MODES).T
 
     def mix_back(e):
-        for half in range(nh):
-            arrive(e, half)
         grad_modes[...] = own_modes(e)
 
         def step(j, carry):
@@ -513,14 +534,48 @@
             total = total + (mixing[i, o] if back else mixing[o, i]) * values[i]
         return total
 
-    pl.semaphore_wait(barrier, n)
+    def fetch_small():
+        for copy in small:
+            copy.wait_recv()
+        for k, (source, target) in enumerate([(mixv1, mix1), (biasv1, bias1)]):
+            copy = pltpu.make_async_copy(source, target, store_sem.at[k])
+            copy.start()
+            copy.wait()
+
+    def back_block(half, q, offset):
+        field = to_field(3, half, q)
+        x0 = (half * hq + q) * xq
+        block = []
+        for k in range(xq):
+            incoming = (row(field, k) + offset[:, x0 + k]).astype(bf16).astype(f32)
+            signal = incoming * slope[:, x0 + k]
+            block.append((x0 + k, signal))
+        return block
+
+    def packed(block):
+        return jnp.concatenate([s.astype(bf16).reshape(rows, zr) for _, s in block], axis=1)
+
+    def blend_back(start, stop):
+        def step(x, carry):
+            values = [sig[i, x] for i in range(channels)]
+            for o in range(channels):
+                u[o, x] = blend(mix_ref, values, o, True)
+            return carry
+
+        lax.fori_loop(start, stop, step, 0)
+
+    pl.semaphore_wait(barrier, 2 * n - 1)
+    for copy in small:
+        copy.start()
 
     @pl.when(last)
     def _():
-        for copy in small:
-            copy.start()
-
-    send_rows(0, cuts[0])
+        send_rows(0, cuts[0])
+
+    @pl.when(first)
+    def _():
+        send_rows(tail, xr)
+
     for load in loads[:3]:
         load.wait()
     for half in range(nh):
@@ -529,7 +584,7 @@
             x = (half * hq + q) * xq
             block = [act[:, x + k].reshape(rows, zr) for k in range(xq)]
             blocks.append(jnp.concatenate(block, axis=1))
-        to_modes(blocks, 0, half)
+        to_modes(blocks, 0, half, 0)
         send_modes(0, 0, half)
 
     for load in loads[3:]:
@@ -561,19 +616,18 @@
 
     lax.fori_loop(0, jl, mix, 0)
     mt_send[0] = mixed()
+    modes_copy(0).start()
 
     @pl.when(last)
     def _():
-        modes_copy(0).start()
-
-    send_rows(cuts[0], cuts[1])
+        send_rows(cuts[0], cuts[1])
+
     send_cells(mt_send[0], 0, 1)
 
     @pl.when(last)
     def _():
         for half in range(nh):
             arrive(1, half)
-
             blocks = []
             for q in range(hq):
                 field = to_field(1, half, q)
@@ -584,25 +638,64 @@
                     sig[:, x0 + k] = signal
                     block.append(signal.astype(bf16).reshape(rows, zr))
                 blocks.append(jnp.concatenate(block, axis=1))
-            to_modes(blocks, 1, half)
+            to_modes(blocks, 1, half, 0)
             send_modes(1, 2, half)
+
+        modes_copy(0).wait_recv()
+        table = [
+            sp[i, nh - 1, :, hq - 1].reshape(nx * 16, cl * MODES) for i in range(2)
+        ]
+        p_ref[3, nh - 1, :, hq - 1] = cells_of(table, mt_recv[0]).reshape(nx, 16, lanes)
+        send_quarter(lambda d, h: p_ref.at[3, nh - 1, d, hq - 1], 5, nh - 1, hq - 1)
+        fetch_small()
+
+        for half in range(nh):
+            arrive(2, half)
         mix_back(2)
         mt_send[1] = mixed()
         modes_copy(1).start()
-        for x in range(cuts[1], xr):
-            row_copy(x).start()
+        send_rows(cuts[1], tail)
         send_cells(mt_send[1], 1, 3)
+
+        blend_back(0, xr)
+        arrive_quarter(5, nh - 1, hq - 1)
+        for x in range(tail, xr):
+            row_copy(x).wait_recv()
+        field = to_field(5, nh - 1, hq - 1)
+        for k in range(xq):
+            values = [act1[i, tail + k].astype(f32) for i in range(channels)]
+            here = row(field, k)
+            for o in range(channels):
+                slope[o, tail + k] = slope_of(here[o] + blend(mix1, values, o, False) + bias1[0, o])
+        arrive(3, nh - 1)
+        to_modes([packed(back_block(nh - 1, hq - 1, u))], 2, nh - 1, hq - 1)
+        lax.fori_loop(0, n, send_tail, 0)
+        send_rows(tail, xr)
+
+    def ahead_quarter(half, q):
+        field = to_field(2, half, q)
+        x0 = (half * hq + q) * xq
+        for k in range(xq):
+            row_copy(x0 + k).wait_recv()
+            values = [act1[i, x0 + k].astype(f32) for i in range(channels)]
+            here = row(field, k)
+            signals = []
+            for o in range(channels):
+                pre = here[o] + blend(mix1, values, o, False) + bias1[0, o]
+                signals.append(cot[o, x0 + k].astype(f32) * slope_of(pre))
+            for i in range(channels):
+                v[i, x0 + k] = blend(mix1, signals, i, True)
+
+    def kept(block):
+        for x, signal in block:
+            sig[:, x] = signal
+        return block
 
     @pl.when(first)
     def _():
         modes_copy(0).wait_recv()
         send_cells(mt_recv[0], 1, 2)
-        for copy in small:
-            copy.wait_recv()
-        for k, (source, target) in enumerate([(mixv1, mix1), (biasv1, bias1)]):
-            copy = pltpu.make_async_copy(source, target, store_sem.at[k])
-            copy.start()
-            copy.wait()
+        fetch_small()
         for half in range(nh):
             arrive(1, half)
 
@@ -615,61 +708,32 @@
 
             lax.fori_loop(0, hq, step, 0)
 
-        def ahead_quarter(half, q):
-            field = to_field(2, half, q)
-            x0 = (half * hq + q) * xq
-            for k in range(xq):
-                row_copy(x0 + k).wait_recv()
-                values = [act1[i, x0 + k].astype(f32) for i in range(channels)]
-                here = row(field, k)
-                signals = []
-                for o in range(channels):
-                    pre = here[o] + blend(mix1, values, o, False) + bias1[0, o]
-                    signals.append(cot[o, x0 + k].astype(f32) * slope_of(pre))
-                for i in range(channels):
-                    v[i, x0 + k] = blend(mix1, signals, i, True)
-
-        def back_half(half):
-            blocks = []
-            for q in range(hq):
-                field = to_field(3, half, q)
-                x0 = (half * hq + q) * xq
-                block = []
-                for k in range(xq):
-                    incoming = (row(field, k) + v[:, x0 + k]).astype(bf16).astype(f32)
-                    signal = incoming * slope[:, x0 + k]
-                    sig[:, x0 + k] = signal
-                    block.append(signal.astype(bf16).reshape(rows, zr))
-                blocks.append(jnp.concatenate(block, axis=1))
-            to_modes(blocks, 1, half)
-            send_modes(1, 4, half)
-
         for half in range(nh):
             arrive(2, half)
-        quarters = [(half, q) for half in range(nh) for q in range(hq)]
+        quarters = [(half, q) for half in range(nh) for q in range(hq)][:-1]
         early = cuts[1] // xq
         for half, q in quarters[:early]:
             ahead_quarter(half, q)
         modes_copy(1).wait_recv()
         send_cells(mt_recv[1], 2, 3)
+        for half in range(nh):
+            arrive(3, half)
+        for half in range(nh - 1):
+            to_modes([packed(kept(back_block(half, q, v))) for q in range(hq)], 1, half, 0)
+            send_modes(1, 4, half)
         for half, q in quarters[early:]:
             ahead_quarter(half, q)
-            if (half, q) == (nh - 1, 0):
-                for back in range(nh):
-                    arrive(3, back)
-                for back in range(nh - 1):
-                    back_half(back)
-        back_half(nh - 1)
+        for q in range(hq - 1):
+            to_modes([packed(kept(back_block(nh - 1, q, v)))], 1, nh - 1, q)
+            send_quarter(lambda d, h: s_ref.at[1, nh - 1, h * nx + d, q], 4, nh - 1, q)
+        for half in range(nh - 1):
+            arrive(4, half)
+        for q in range(hq - 1):
+            arrive_quarter(4, nh - 1, q)
+        await_block(r_ref.at[4, nh - 1, :, hq - 1], tail_recv.at[0])
         mix_back(4)
         send_cells(mixed(), 3, 5)
-
-    def pointwise_back(x, carry):
-        values = [sig[i, x] for i in range(channels)]
-        for o in range(channels):
-            u[o, x] = blend(mix_ref, values, o, True)
-        return carry
-
-    lax.fori_loop(0, xr, pointwise_back, 0)
+        blend_back(0, tail)
 
     def weight_grad(j, carry):
         for c in range(cl):
@@ -679,33 +743,58 @@
 
     lax.fori_loop(0, jl, weight_grad, 0)
     e = 3 + 2 * (1 - seg)
+
+    @pl.when(last)
+    def _():
+        for half in range(nh - 1):
+            arrive(3, half)
+
+    @pl.when(first)
+    def _():
+        for half in range(nh - 1):
+            arrive(5, half)
+
     for half in range(nh - 1):
-        arrive(e, half)
         for q in range(hq):
             field = to_field(e, half, q)
             x0 = (half * hq + q) * xq
             for k in range(xq):
                 out[:, x0 + k] = (row(field, k) + u[:, x0 + k]).astype(bf16)
-    done = (nh - 1) * hq * xq
-    rest_ref[...] = u[:, done:]
-    arrive(e, nh - 1)
-    cells_ref[...] = r_ref[e, nh - 1]
-    for e in range(4):
-        sent(e)
 
     @pl.when(first)
     def _():
-        sent(4)
-        sent(5)
+        ahead_quarter(nh - 1, hq - 1)
+        kept(back_block(nh - 1, hq - 1, v))
+        blend_back(tail, xr)
+        arrive(5, nh - 1)
+
+    rest_ref[...] = u[:, (nh - 1) * hq * xq :]
+    cells_ref[...] = r_ref[e, nh - 1]
+    for half in range(nh):
+        for k in range(4):
+            sent(k, half)
+    for copy in small:
+        copy.wait_send()
+    modes_copy(0).wait_send()
+
+    @pl.when(first)
+    def _():
+        for half in range(nh - 1):
+            sent(4, half)
+        for q in range(hq - 1):
+            sent_quarter(4, nh - 1, q)
+        for half in range(nh):
+            sent(5, half)
+        for x in range(tail, xr):
+            row_copy(x).wait_send()
 
     @pl.when(last)
     def _():
-        for copy in small:
-            copy.wait_send()
+        sent_quarter(5, nh - 1, hq - 1)
+        modes_copy(1).wait_send()
+        await_block(r_ref.at[4, nh - 1, :, hq - 1], tail_send.at[0])
         for x in range(xr):
             row_copy(x).wait_send()
-        for k in range(2):
-            modes_copy(k).wait_send()
 
 
 def finish_kernel(
@@ -765,7 +854,7 @@
         np.concatenate([bzf[0], bzf[1]], axis=1),
         np.concatenate([bzi[0], bzi[0], bzi[1]], axis=0),
         halves(bxf),
-        halves(sp),
+        halves(sp).reshape(2, nh, nx, hq, 16, cl * MODES),
     ]
     weights, mixing = spectral_weights[0], pointwise[0]
     vmem = pl.BlockSpec(memory_space=pltpu.VMEM)
@@ -782,7 +871,7 @@
         pltpu.VMEM((2, ny * lanes, rows), bf16),
         pltpu.VMEM((xq * zr, 2 * nx * 16), bf16),
         pltpu.VMEM((2, cl * MODES, nh * n * hq * 16), bf16),
-        pltpu.VMEM((2, nh * nx * hq * 16, cl * MODES), bf16),
+        pltpu.VMEM((2, nh, nx, hq, 16, cl * MODES), bf16),
         pltpu.VMEM(grid, f32), pltpu.VMEM(grid, f32), pltpu.VMEM(grid, f32), pltpu.VMEM(grid, f32),
         pltpu.VMEM((jl, channels, cl * MODES), f32),
         pltpu.VMEM((jl, channels, cl * MODES), f32),
@@ -791,11 +880,11 @@
         pltpu.VMEM((2, cl * MODES, lanes), f32),
         pltpu.VMEM(mixing.shape, f32), pltpu.VMEM(channel_bias.shape, f32),
         pltpu.SMEM(mixing.shape, f32), pltpu.SMEM(channel_bias.shape, f32),
-        pltpu.VMEM((2, nh, n, hq, 16, lanes), bf16),
+        pltpu.VMEM((3, nh, n, hq, 16, lanes), bf16),
         pltpu.VMEM((4, nh, nx, hq, 16, lanes), bf16),
         pltpu.VMEM((6, nh, n, hq, 16, lanes), bf16),
         dma((9,)), dma((6, nh)), dma((6, nh)),
-        dma((xr,)), dma((xr,)), dma((4,)), dma((4,)), dma((2,)),
+        dma((xr,)), dma((xr,)), dma((4,)), dma((4,)), dma((2,)), dma((1,)), dma((1,)),
     ]
     parts = pl.pallas_call(
         functools.partial(relay_kernel, nx, ny, xq, (3, 9)),
@@ -807,7 +896,7 @@
             jax.ShapeDtypeStruct((2, rows, ny * lanes), bf16),
             jax.ShapeDtypeStruct((3 * nx * 16, xq * zr), bf16),
         ),
-        in_specs=[hbm, hbm, hbm, smem, smem, vmem, vmem] + [hbm] * len(tables),
+        in_specs=[hbm, hbm, hbm, smem, smem] + [hbm] * (2 + len(tables)),
         out_specs=[vmem] * 6,
         scratch_shapes=scratch,
         compiler_params=pltpu.CompilerParams(
@@ -817,8 +906,11 @@
             flops=4 * 10**9, bytes_accessed=2 * 10**7, transcendentals=10**7
         ),
     )(
-        inputs, cotangent, weights, mixing, channel_bias, mixing, channel_bias,
-        *[pltpu.with_memory_space_constraint(jnp.asarray(table), pltpu.HBM) for table in tables],
+        inputs, cotangent, weights, mixing, channel_bias,
+        *[
+            pltpu.with_memory_space_constraint(jnp.asarray(table), pltpu.HBM)
+            for table in [mixing, channel_bias] + tables
+        ],
     )
     input_grad, weight_grad = pl.pallas_call(
         functools.partial(finish_kernel, nx, ny, xq),

time: 78.7 us -> 71.1 us (0.903)
  Pallas kernels: 76.3 us -> 70 us
  local copies, waits for them, and re-layouts: 1.33 us -> 0 us
    pallas_call x1, Pallas kernels: 74.1 us -> 67.8 us  [two_section_body(): pl.pallas_call(functools.partial(relay_kernel, nx, ny, xq, (3, 9)), out_s...]
    unnamed x4 -> x0, local copies, waits for them, and re-layouts: 1.33 us -> none
where the time goes in v3:
time: 71.1 us; the launch traced here: 70.8 us
  Pallas kernels  70 us (98%)
  between operations  0.82 us (1%)
    pallas_call x1, Pallas kernels, two_section_body(): pl.pallas_call(functools.partial(relay_kernel, nx, ny, xq, (3, 9)), out_s...  67.8 us
    pallas_call x1, Pallas kernels, two_section_body(): pl.pallas_call(functools.partial(finish_kernel, nx, ny, xq), out_shape=(j...  2.16 us

profile of v3, /device:TPU:0, one launch (start us, length us, event | category | flops | bytes accessed | tf_op | source)
XLA Modules:
  0.0 70.8 jit_solution(18418674895072083442)
XLA Ops:
  0.6 67.8 %shard_map.122 = (bf16[8,8,64,128]{3,2,1,0:T(8,128)(2,1)S(1)}, f32[8,8,64,128]{3,2,1,0:T(8,128)S(1)}, bf16[16,2,16,128]{3,2,1,0:T(8,128)(2,1)S(1)}, f32[16,4,8,8...) custom-call(bf16[8,16,64,128]{3,2,1,0:T(8,128)(2,1)} %bitcast.5, ...), custom_call_target="tpu_custom_call" | custom-call | flops 4000000000 | bytes 20000000 | tf_op jit(solution)/shard_map/pallas_call | solution.py:889
  68.5 2.2 %shard_map.123 = (bf16[8,16,64,128]{3,2,1,0:T(8,128)(2,1)}, f32[16,4,8,8,32]{4,3,2,1,0:T(8,128)}) custom-call(bf16[8,8,64,128]{3,2,1,0:T(8,128)(2,1)S(1)} %get-tuple-element.10.done_ref, f32[8,8,64,128]{3,2,1,0:T(8,128)S(1)} %get-tuple-element.11.rest_ref, bf16[16,2,16,128]{3,2,1,0:T(8,128)(2,1)S(1)} %get-tuple-element.12.cells_ref, ...), custom_call_target="tpu_custom_call" | custom-call | flops 1000000000 | bytes 10000000 | tf_op jit(solution)/shard_map/pallas_call | solution.py:915

commit v4 on v3

--- a/solution.py
+++ b/solution.py
@@ -380,7 +380,7 @@
     nh, hq = r_ref.shape[1], r_ref.shape[3]
     lanes = jl * channels
     rows = channels * yr
-    tail = xr - xq
+    tail = xr - hq * xq
     gx, gy, seg = lax.axis_index("gx"), lax.axis_index("gy"), lax.axis_index("segment")
     me = gx * ny + gy
     mine = gy * nx + gx
@@ -450,15 +450,11 @@
     def send_half(source, e, half):
         send(source, r_ref.at[e, half, mine], send_sem.at[e, half], recv_sem.at[e, half])
 
-    def send_quarter(source, e, half, q):
-        send(source, r_ref.at[e, half, mine, q], send_sem.at[e, half], recv_sem.at[e, half])
-
     def send_tail(k, carry):
         peer = lax.rem(me + k, n)
         d, h = peer // ny, lax.rem(peer, ny)
         pltpu.make_async_remote_copy(
-            src_ref=s_ref.at[2, nh - 1, h * nx + d, hq - 1],
-            dst_ref=r_ref.at[4, nh - 1, mine, hq - 1],
+            src_ref=s_ref.at[2, nh - 1, h * nx + d], dst_ref=r_ref.at[4, nh - 1, mine],
             send_sem=tail_send.at[0], recv_sem=tail_recv.at[0],
             device_id={"segment": 0, "gx": d, "gy": h}, device_id_type=mesh_ids,
         ).start()
@@ -470,16 +466,10 @@
     def arrive(e, half):
         await_block(r_ref.at[e, half, pl.ds(0, n - 1)], recv_sem.at[e, half])
 
-    def arrive_quarter(e, half, q):
-        await_block(r_ref.at[e, half, pl.ds(0, n - 1), q], recv_sem.at[e, half])
-
     def sent(e, half):
         await_block(r_ref.at[e, half, pl.ds(0, n - 1)], send_sem.at[e, half])
 
-    def sent_quarter(e, half, q):
-        await_block(r_ref.at[e, half, pl.ds(0, n - 1), q], send_sem.at[e, half])
-
-    def to_modes(blocks, k, half, q0):
+    def to_modes(blocks, k, half):
         parts = []
         for block in blocks:
             g = dot(block, bzf[...])
@@ -490,7 +480,7 @@
         for q in range(len(blocks)):
             for h in range(ny):
                 part = t[q * nx * 16 : (q + 1) * nx * 16, h * lanes : (h + 1) * lanes]
-                s_ref[k, half, h * nx : (h + 1) * nx, q0 + q] = part.reshape(nx, 16, lanes)
+                s_ref[k, half, h * nx : (h + 1) * nx, q] = part.reshape(nx, 16, lanes)
 
     def to_field(e, half, q):
         return field_of(lambda h: r_ref[e, half, h * nx : (h + 1) * nx, q], ny, ky, bzi)
@@ -501,26 +491,29 @@
     def send_modes(k, e, half):
         send_half(lambda d, h: s_ref.at[k, half, h * nx + d], e, half)
 
-    def own_modes(e):
-        block = r_ref[e].reshape(nh * n * hq * 16, lanes)
-        own = dot(bx[0], block) + dot(bx[1], block)
+    def own_modes(e, await_half):
+        own = None
+        for half in range(nh):
+            await_half(half)
+            block = r_ref[e, half].reshape(n * hq * 16, lanes)
+            part = slice(half * n * hq * 16, (half + 1) * n * hq * 16)
+            term = dot(bx[0, :, part], block) + dot(bx[1, :, part], block)
+            own = term if own is None else own + term
         return own.T.reshape(jl, channels, cl * MODES)
 
-    def cells_of(table, mt):
+    def send_cells(mt, k, e, halves):
         top, rest = split(mt)
-        return (dot(table[0], top) + dot(table[1], top) + dot(table[0], rest)).astype(bf16)
-
-    def send_cells(mt, k, e):
-        table = [sp[i].reshape(nh * nx * hq * 16, cl * MODES) for i in range(2)]
-        p_ref[k] = cells_of(table, mt).reshape(nh, nx, hq, 16, lanes)
-        for half in range(nh):
+        for half in halves:
+            table = [sp[i, half].reshape(nx * hq * 16, cl * MODES) for i in range(2)]
+            cells = dot(table[0], top) + dot(table[1], top) + dot(table[0], rest)
+            p_ref[k, half] = cells.astype(bf16).reshape(nx, hq, 16, lanes)
             send_half(lambda d, h: p_ref.at[k, half, d], e, half)
 
     def mixed():
         return m_ref[...].reshape(lanes, cl * MODES).T
 
-    def mix_back(e):
-        grad_modes[...] = own_modes(e)
+    def mix_back(e, await_half):
+        grad_modes[...] = own_modes(e, await_half)
 
         def step(j, carry):
             m_ref[j] = jnp.sum(wd[j] * grad_modes[j][None], axis=1)
@@ -564,18 +557,6 @@
 
         lax.fori_loop(start, stop, step, 0)
 
-    pl.semaphore_wait(barrier, 2 * n - 1)
-    for copy in small:
-        copy.start()
-
-    @pl.when(last)
-    def _():
-        send_rows(0, cuts[0])
-
-    @pl.when(first)
-    def _():
-        send_rows(tail, xr)
-
     for load in loads[:3]:
         load.wait()
     for half in range(nh):
@@ -584,7 +565,20 @@
             x = (half * hq + q) * xq
             block = [act[:, x + k].reshape(rows, zr) for k in range(xq)]
             blocks.append(jnp.concatenate(block, axis=1))
-        to_modes(blocks, 0, half, 0)
+        to_modes(blocks, 0, half)
+        if half == 0:
+            pl.semaphore_wait(barrier, 2 * n - 1)
+            for copy in small:
+                copy.start()
+
+            @pl.when(last)
+            def _():
+                send_rows(0, cuts[0])
+
+            @pl.when(first)
+            def _():
+                send_rows(tail, xr)
+
         send_modes(0, 0, half)
 
     for load in loads[3:]:
@@ -605,9 +599,7 @@
 
     lax.fori_loop(0, xr, pointwise, 0)
 
-    for half in range(nh):
-        arrive(0, half)
-    in_modes[...] = own_modes(0)
+    in_modes[...] = own_modes(0, lambda half: arrive(0, half))
 
     def mix(j, carry):
         own = in_modes[j]
@@ -622,7 +614,7 @@
     def _():
         send_rows(cuts[0], cuts[1])
 
-    send_cells(mt_send[0], 0, 1)
+    send_cells(mt_send[0], 0, 1, range(nh))
 
     @pl.when(last)
     def _():
@@ -638,39 +630,36 @@
                     sig[:, x0 + k] = signal
                     block.append(signal.astype(bf16).reshape(rows, zr))
                 blocks.append(jnp.concatenate(block, axis=1))
-            to_modes(blocks, 1, half, 0)
+            to_modes(blocks, 1, half)
             send_modes(1, 2, half)
 
         modes_copy(0).wait_recv()
-        table = [
-            sp[i, nh - 1, :, hq - 1].reshape(nx * 16, cl * MODES) for i in range(2)
-        ]
-        p_ref[3, nh - 1, :, hq - 1] = cells_of(table, mt_recv[0]).reshape(nx, 16, lanes)
-        send_quarter(lambda d, h: p_ref.at[3, nh - 1, d, hq - 1], 5, nh - 1, hq - 1)
+        send_cells(mt_recv[0], 3, 5, [nh - 1])
         fetch_small()
 
-        for half in range(nh):
-            arrive(2, half)
-        mix_back(2)
+        mix_back(2, lambda half: arrive(2, half))
         mt_send[1] = mixed()
         modes_copy(1).start()
-        send_rows(cuts[1], tail)
-        send_cells(mt_send[1], 1, 3)
+        send_rows(cuts[1], cuts[2])
+        send_cells(mt_send[1], 1, 3, reversed(range(nh)))
 
         blend_back(0, xr)
-        arrive_quarter(5, nh - 1, hq - 1)
         for x in range(tail, xr):
             row_copy(x).wait_recv()
-        field = to_field(5, nh - 1, hq - 1)
-        for k in range(xq):
-            values = [act1[i, tail + k].astype(f32) for i in range(channels)]
-            here = row(field, k)
-            for o in range(channels):
-                slope[o, tail + k] = slope_of(here[o] + blend(mix1, values, o, False) + bias1[0, o])
+        arrive(5, nh - 1)
+        for q in range(hq):
+            field = to_field(5, nh - 1, q)
+            x0 = tail + q * xq
+            for k in range(xq):
+                values = [act1[i, x0 + k].astype(f32) for i in range(channels)]
+                here = row(field, k)
+                for o in range(channels):
+                    pre = here[o] + blend(mix1, values, o, False) + bias1[0, o]
+                    slope[o, x0 + k] = slope_of(pre)
         arrive(3, nh - 1)
-        to_modes([packed(back_block(nh - 1, hq - 1, u))], 2, nh - 1, hq - 1)
+        to_modes([packed(back_block(nh - 1, q, u)) for q in range(hq)], 2, nh - 1)
         lax.fori_loop(0, n, send_tail, 0)
-        send_rows(tail, xr)
+        send_rows(cuts[2], xr)
 
     def ahead_quarter(half, q):
         field = to_field(2, half, q)
@@ -694,7 +683,7 @@
     @pl.when(first)
     def _():
         modes_copy(0).wait_recv()
-        send_cells(mt_recv[0], 1, 2)
+        send_cells(mt_recv[0], 1, 2, range(nh))
         fetch_small()
         for half in range(nh):
             arrive(1, half)
@@ -710,30 +699,29 @@
 
         for half in range(nh):
             arrive(2, half)
-        quarters = [(half, q) for half in range(nh) for q in range(hq)][:-1]
-        early = cuts[1] // xq
-        for half, q in quarters[:early]:
-            ahead_quarter(half, q)
+        for half in range(nh - 1):
+            for q in range(hq):
+                ahead_quarter(half, q)
         modes_copy(1).wait_recv()
-        send_cells(mt_recv[1], 2, 3)
-        for half in range(nh):
+        send_cells(mt_recv[1], 2, 3, range(nh))
+        for half in range(nh - 1):
             arrive(3, half)
-        for half in range(nh - 1):
-            to_modes([packed(kept(back_block(half, q, v))) for q in range(hq)], 1, half, 0)
+            to_modes([packed(kept(back_block(half, q, v))) for q in range(hq)], 1, half)
             send_modes(1, 4, half)
-        for half, q in quarters[early:]:
-            ahead_quarter(half, q)
+        blend_back(0, tail)
+        arrive(3, nh - 1)
         for q in range(hq - 1):
-            to_modes([packed(kept(back_block(nh - 1, q, v)))], 1, nh - 1, q)
-            send_quarter(lambda d, h: s_ref.at[1, nh - 1, h * nx + d, q], 4, nh - 1, q)
-        for half in range(nh - 1):
-            arrive(4, half)
-        for q in range(hq - 1):
-            arrive_quarter(4, nh - 1, q)
-        await_block(r_ref.at[4, nh - 1, :, hq - 1], tail_recv.at[0])
-        mix_back(4)
-        send_cells(mixed(), 3, 5)
-        blend_back(0, tail)
+            ahead_quarter(nh - 1, q)
+            kept(back_block(nh - 1, q, v))
+
+        def await_half(half):
+            if half < nh - 1:
+                arrive(4, half)
+            else:
+                await_block(r_ref.at[4, half], tail_recv.at[0])
+
+        mix_back(4, await_half)
+        send_cells(mixed(), 3, 5, range(nh))
 
     def weight_grad(j, carry):
         for c in range(cl):
@@ -781,8 +769,6 @@
     def _():
         for half in range(nh - 1):
             sent(4, half)
-        for q in range(hq - 1):
-            sent_quarter(4, nh - 1, q)
         for half in range(nh):
             sent(5, half)
         for x in range(tail, xr):
@@ -790,9 +776,9 @@
 
     @pl.when(last)
     def _():
-        sent_quarter(5, nh - 1, hq - 1)
+        sent(5, nh - 1)
         modes_copy(1).wait_send()
-        await_block(r_ref.at[4, nh - 1, :, hq - 1], tail_send.at[0])
+        await_block(r_ref.at[4, nh - 1], tail_send.at[0])
         for x in range(xr):
             row_copy(x).wait_send()
 
@@ -887,7 +873,7 @@
         dma((xr,)), dma((xr,)), dma((4,)), dma((4,)), dma((2,)), dma((1,)), dma((1,)),
     ]
     parts = pl.pallas_call(
-        functools.partial(relay_kernel, nx, ny, xq, (3, 9)),
+        functools.partial(relay_kernel, nx, ny, xq, (3, 9, 12)),
         out_shape=(
             jax.ShapeDtypeStruct(done, bf16),
             jax.ShapeDtypeStruct(left, f32),

time: 71.1 us -> 68.1 us (0.958)
  Pallas kernels: 70 us -> 67.1 us
    pallas_call x1, Pallas kernels: 67.8 us -> 65 us  [two_section_body(): pl.pallas_call(functools.partial(relay_kernel, nx, ny, xq, (3, 9, 12)), o...]
where the time goes in v4:
time: 68.1 us; the launch traced here: 67.9 us
  Pallas kernels  67.1 us (99%)
  between operations  0.82 us (1%)
    pallas_call x1, Pallas kernels, two_section_body(): pl.pallas_call(functools.partial(relay_kernel, nx, ny, xq, (3, 9, 12)), o...  65 us
    pallas_call x1, Pallas kernels, two_section_body(): pl.pallas_call(functools.partial(finish_kernel, nx, ny, xq), out_shape=(j...  2.16 us

profile of v4, /device:TPU:0, one launch (start us, length us, event | category | flops | bytes accessed | tf_op | source)
XLA Modules:
  0.0 67.9 jit_solution(16594842008838456637)
XLA Ops:
  0.6 65.0 %shard_map.122 = (bf16[8,8,64,128]{3,2,1,0:T(8,128)(2,1)S(1)}, f32[8,8,64,128]{3,2,1,0:T(8,128)S(1)}, bf16[16,2,16,128]{3,2,1,0:T(8,128)(2,1)S(1)}, f32[16,4,8,8...) custom-call(bf16[8,16,64,128]{3,2,1,0:T(8,128)(2,1)} %bitcast.5, ...), custom_call_target="tpu_custom_call" | custom-call | flops 4000000000 | bytes 20000000 | tf_op jit(solution)/shard_map/pallas_call | solution.py:875
  65.6 2.2 %shard_map.123 = (bf16[8,16,64,128]{3,2,1,0:T(8,128)(2,1)}, f32[16,4,8,8,32]{4,3,2,1,0:T(8,128)}) custom-call(bf16[8,8,64,128]{3,2,1,0:T(8,128)(2,1)S(1)} %get-tuple-element.10.done_ref, f32[8,8,64,128]{3,2,1,0:T(8,128)S(1)} %get-tuple-element.11.rest_ref, bf16[16,2,16,128]{3,2,1,0:T(8,128)(2,1)S(1)} %get-tuple-element.12.cells_ref, ...), custom_call_target="tpu_custom_call" | custom-call | flops 1000000000 | bytes 10000000 | tf_op jit(solution)/shard_map/pallas_call | solution.py:901

commit v5 on v4

--- a/solution.py
+++ b/solution.py
@@ -372,7 +372,7 @@
     u, v, slope, sig, in_modes, grad_modes, m_ref, mt_send, mt_recv,
     mixv1, biasv1, mix1, bias1, s_ref, p_ref, r_ref,
     load_sem, send_sem, recv_sem, row_send, row_recv, small_send, small_recv, store_sem,
-    tail_send, tail_recv,
+    tail_send, tail_recv, pair_send, pair_recv,
 ):
     channels, xr, yr, zr = act.shape
     n = nx * ny
@@ -381,6 +381,7 @@
     lanes = jl * channels
     rows = channels * yr
     tail = xr - hq * xq
+    late = xr - xq
     gx, gy, seg = lax.axis_index("gx"), lax.axis_index("gy"), lax.axis_index("segment")
     me = gx * ny + gy
     mine = gy * nx + gx
@@ -449,6 +450,39 @@
 
     def send_half(source, e, half):
         send(source, r_ref.at[e, half, mine], send_sem.at[e, half], recv_sem.at[e, half])
+
+    def send_along(source, e, half):
+        def begin(k, carry):
+            d = lax.rem(gx + k, nx)
+            pltpu.make_async_remote_copy(
+                src_ref=source(d), dst_ref=r_ref.at[e, half, mine],
+                send_sem=send_sem.at[e, half], recv_sem=recv_sem.at[e, half],
+                device_id={"gx": d}, device_id_type=mesh_ids,
+            ).start()
+            return carry
+
+        lax.fori_loop(1, nx, begin, 0)
+        r_ref[e, half, mine] = source(gx)[...]
+
+    def pair_copy(e, half):
+        block = r_ref.at[e, half, pl.ds(gy * nx, nx)]
+        return pltpu.make_async_remote_copy(
+            src_ref=block, dst_ref=block,
+            send_sem=pair_send.at[e, half], recv_sem=pair_recv.at[e, half],
+            device_id={"gy": 1 - gy}, device_id_type=mesh_ids,
+        )
+
+    def forward(e, halves):
+        for half in halves:
+            await_block(r_ref.at[e, half, pl.ds(0, nx - 1)], recv_sem.at[e, half])
+            pair_copy(e, half).start()
+
+    def land(e, half):
+        await_block(r_ref.at[e, half, pl.ds(0, nx)], pair_recv.at[e, half])
+
+    def sent_along(e, half):
+        await_block(r_ref.at[e, half, pl.ds(0, nx - 1)], send_sem.at[e, half])
+        await_block(r_ref.at[e, half, pl.ds(0, nx)], pair_send.at[e, half])
 
     def send_tail(k, carry):
         peer = lax.rem(me + k, n)
@@ -507,7 +541,7 @@
             table = [sp[i, half].reshape(nx * hq * 16, cl * MODES) for i in range(2)]
             cells = dot(table[0], top) + dot(table[1], top) + dot(table[0], rest)
             p_ref[k, half] = cells.astype(bf16).reshape(nx, hq, 16, lanes)
-            send_half(lambda d, h: p_ref.at[k, half, d], e, half)
+            send_along(lambda d: p_ref.at[k, half, d], e, half)
 
     def mixed():
         return m_ref[...].reshape(lanes, cl * MODES).T
@@ -557,6 +591,18 @@
 
         lax.fori_loop(start, stop, step, 0)
 
+    pl.semaphore_wait(barrier, 2 * n - 1)
+    for copy in small:
+        copy.start()
+
+    @pl.when(last)
+    def _():
+        send_rows(0, cuts[0])
+
+    @pl.when(first)
+    def _():
+        send_rows(tail, xr)
+
     for load in loads[:3]:
         load.wait()
     for half in range(nh):
@@ -566,19 +612,6 @@
             block = [act[:, x + k].reshape(rows, zr) for k in range(xq)]
             blocks.append(jnp.concatenate(block, axis=1))
         to_modes(blocks, 0, half)
-        if half == 0:
-            pl.semaphore_wait(barrier, 2 * n - 1)
-            for copy in small:
-                copy.start()
-
-            @pl.when(last)
-            def _():
-                send_rows(0, cuts[0])
-
-            @pl.when(first)
-            def _():
-                send_rows(tail, xr)
-
         send_modes(0, 0, half)
 
     for load in loads[3:]:
@@ -618,8 +651,9 @@
 
     @pl.when(last)
     def _():
+        forward(1, range(nh))
         for half in range(nh):
-            arrive(1, half)
+            land(1, half)
             blocks = []
             for q in range(hq):
                 field = to_field(1, half, q)
@@ -646,7 +680,8 @@
         blend_back(0, xr)
         for x in range(tail, xr):
             row_copy(x).wait_recv()
-        arrive(5, nh - 1)
+        forward(5, [nh - 1])
+        land(5, nh - 1)
         for q in range(hq):
             field = to_field(5, nh - 1, q)
             x0 = tail + q * xq
@@ -656,7 +691,8 @@
                 for o in range(channels):
                     pre = here[o] + blend(mix1, values, o, False) + bias1[0, o]
                     slope[o, x0 + k] = slope_of(pre)
-        arrive(3, nh - 1)
+        forward(3, reversed(range(nh)))
+        land(3, nh - 1)
         to_modes([packed(back_block(nh - 1, q, u)) for q in range(hq)], 2, nh - 1)
         lax.fori_loop(0, n, send_tail, 0)
         send_rows(cuts[2], xr)
@@ -685,8 +721,9 @@
         modes_copy(0).wait_recv()
         send_cells(mt_recv[0], 1, 2, range(nh))
         fetch_small()
+        forward(1, range(nh))
         for half in range(nh):
-            arrive(1, half)
+            land(1, half)
 
             def step(q, carry):
                 field = to_field(1, half, q)
@@ -697,19 +734,21 @@
 
             lax.fori_loop(0, hq, step, 0)
 
+        forward(2, range(nh))
         for half in range(nh):
-            arrive(2, half)
+            land(2, half)
         for half in range(nh - 1):
             for q in range(hq):
                 ahead_quarter(half, q)
         modes_copy(1).wait_recv()
         send_cells(mt_recv[1], 2, 3, range(nh))
+        forward(3, range(nh))
         for half in range(nh - 1):
-            arrive(3, half)
+            land(3, half)
             to_modes([packed(kept(back_block(half, q, v))) for q in range(hq)], 1, half)
             send_modes(1, 4, half)
         blend_back(0, tail)
-        arrive(3, nh - 1)
+        land(3, nh - 1)
         for q in range(hq - 1):
             ahead_quarter(nh - 1, q)
             kept(back_block(nh - 1, q, v))
@@ -722,6 +761,12 @@
 
         mix_back(4, await_half)
         send_cells(mixed(), 3, 5, range(nh))
+        if hq > 1:
+            blend_back(tail, late)
+        for target, e in ((v, 2), (u, 3)):
+            field = to_field(e, nh - 1, hq - 1)
+            for k in range(xq):
+                target[:, late + k] = row(field, k)
 
     def weight_grad(j, carry):
         for c in range(cl):
@@ -735,32 +780,50 @@
     @pl.when(last)
     def _():
         for half in range(nh - 1):
-            arrive(3, half)
+            land(3, half)
 
     @pl.when(first)
     def _():
-        for half in range(nh - 1):
-            arrive(5, half)
-
-    for half in range(nh - 1):
-        for q in range(hq):
+        forward(5, range(nh))
+        for half in range(nh):
+            land(5, half)
+
+    for half in range(nh):
+        for q in range(hq if half < nh - 1 else hq - 1):
             field = to_field(e, half, q)
             x0 = (half * hq + q) * xq
             for k in range(xq):
                 out[:, x0 + k] = (row(field, k) + u[:, x0 + k]).astype(bf16)
+    cells_ref[...] = r_ref[e, nh - 1, :, hq - 1 :]
 
     @pl.when(first)
     def _():
-        ahead_quarter(nh - 1, hq - 1)
-        kept(back_block(nh - 1, hq - 1, v))
-        blend_back(tail, xr)
-        arrive(5, nh - 1)
-
-    rest_ref[...] = u[:, (nh - 1) * hq * xq :]
-    cells_ref[...] = r_ref[e, nh - 1]
+        def step(k, carry):
+            x = late + k
+            row_copy(x).wait_recv()
+            values = [act1[i, x].astype(f32) for i in range(channels)]
+            signals = []
+            for o in range(channels):
+                pre = v[o, x] + blend(mix1, values, o, False) + bias1[0, o]
+                signals.append(cot[o, x].astype(f32) * slope_of(pre))
+            here = []
+            for i in range(channels):
+                incoming = u[i, x] + blend(mix1, signals, i, True)
+                here.append(incoming.astype(bf16).astype(f32) * slope[i, x])
+            for o in range(channels):
+                rest_ref[o, k] = blend(mix_ref, here, o, True)
+            return carry
+
+        lax.fori_loop(0, xq, step, 0)
+
+    @pl.when(last)
+    def _():
+        rest_ref[...] = u[:, late:]
+
     for half in range(nh):
-        for k in range(4):
-            sent(k, half)
+        sent(0, half)
+        sent_along(1, half)
+        sent_along(3, half)
     for copy in small:
         copy.wait_send()
     modes_copy(0).wait_send()
@@ -770,13 +833,16 @@
         for half in range(nh - 1):
             sent(4, half)
         for half in range(nh):
-            sent(5, half)
+            sent_along(2, half)
+            sent_along(5, half)
         for x in range(tail, xr):
             row_copy(x).wait_send()
 
     @pl.when(last)
     def _():
-        sent(5, nh - 1)
+        for half in range(nh):
+            sent(2, half)
+        sent_along(5, nh - 1)
         modes_copy(1).wait_send()
         await_block(r_ref.at[4, nh - 1], tail_send.at[0])
         for x in range(xr):
@@ -848,8 +914,8 @@
     hbm = pl.BlockSpec(memory_space=pl.ANY)
     dma = pltpu.SemaphoreType.DMA
     grid = inputs.shape
-    done = grid[:1] + ((nh - 1) * hq * xq,) + grid[2:]
-    left = grid[:1] + (hq * xq,) + grid[2:]
+    done = grid[:1] + (xr - xq,) + grid[2:]
+    left = grid[:1] + (xq,) + grid[2:]
     scratch = [
         pltpu.VMEM(grid, bf16), pltpu.VMEM(grid, bf16), pltpu.VMEM(grid, bf16),
         pltpu.VMEM(weights.shape, f32),
@@ -870,14 +936,14 @@
         pltpu.VMEM((4, nh, nx, hq, 16, lanes), bf16),
         pltpu.VMEM((6, nh, n, hq, 16, lanes), bf16),
         dma((9,)), dma((6, nh)), dma((6, nh)),
-        dma((xr,)), dma((xr,)), dma((4,)), dma((4,)), dma((2,)), dma((1,)), dma((1,)),
+        dma((xr,)), dma((xr,)), dma((4,)), dma((4,)), dma((2,)), dma((1,)), dma((1,)), dma((6, nh)), dma((6, nh)),
     ]
     parts = pl.pallas_call(
         functools.partial(relay_kernel, nx, ny, xq, (3, 9, 12)),
         out_shape=(
             jax.ShapeDtypeStruct(done, bf16),
             jax.ShapeDtypeStruct(left, f32),
-            jax.ShapeDtypeStruct((n, hq, 16, lanes), bf16),
+            jax.ShapeDtypeStruct((n, 1, 16, lanes), bf16),
             pltpu.VMEM(weights.shape, f32),
             jax.ShapeDtypeStruct((2, rows, ny * lanes), bf16),
             jax.ShapeDtypeStruct((3 * nx * 16, xq * zr), bf16),
@@ -906,7 +972,7 @@
         ),
         in_specs=[vmem] * 6,
         out_specs=(hbm, hbm),
-        scratch_shapes=[pltpu.VMEM(left, bf16), dma((2 + hq,))],
+        scratch_shapes=[pltpu.VMEM(left, bf16), dma((3,))],
         compiler_params=pltpu.CompilerParams(vmem_limit_bytes=24 * 2**20),
         cost_estimate=pl.CostEstimate(flops=10**9, bytes_accessed=10**7, transcendentals=0),
     )(*parts)

time: 68.1 us -> 69.1 us (1.015); the launches traced: 67.9 us -> 68.1 us
  local copies, waits for them, and re-layouts: 0 us -> 1.58 us
  Pallas kernels: 67.1 us -> 65.7 us
    unnamed x0 -> x2, local copies, waits for them, and re-layouts: none -> 1.58 us
    pallas_call x1, Pallas kernels: 65 us -> 63.7 us  [two_section_body(): pl.pallas_call(functools.partial(relay_kernel, nx, ny, xq, (3, 9, 12)), o...]
where the time goes in v5:
time: 69.1 us; the launch traced here: 68.1 us
  Pallas kernels  65.7 us (95%)
  local copies, waits for them, and re-layouts  1.58 us (2%)
  between operations  0.83 us (1%)
    pallas_call x1, Pallas kernels, two_section_body(): pl.pallas_call(functools.partial(relay_kernel, nx, ny, xq, (3, 9, 12)), o...  63.7 us
    pallas_call x1, Pallas kernels, two_section_body(): pl.pallas_call(functools.partial(finish_kernel, nx, ny, xq), out_shape=(j...  2.03 us
    unnamed x2, local copies, waits for them, and re-layouts  1.58 us

profile of v5, /device:TPU:0, one launch (start us, length us, event | category | flops | bytes accessed | tf_op | source)
XLA Modules:
  0.0 68.1 jit_solution(11938726514175901134)
XLA Ops:
  0.6 0.0 copy-start
  0.6 1.6 %copy-done = bf16[1,8,16,64,128]{4,3,2,1,0:T(8,128)(2,1)S(1)} copy-done((bf16[1,8,16,64,128]{4,3,2,1,0:T(8,128)(2,1)S(1)}, bf16[1,8,16,64,128]{4,3,2,1,0:T(8,128)(2,1)}, u32[]{:S(2)}) %copy-start) | copy-done | bytes 2097176
  2.2 63.7 %shard_map.122 = (bf16[8,12,64,128]{3,2,1,0:T(8,128)(2,1)S(1)}, f32[8,4,64,128]{3,2,1,0:T(8,128)S(1)}, bf16[16,1,16,128]{3,2,1,0:T(8,128)(2,1)S(1)}, f32[16,4,8,...) custom-call(bf16[8,16,64,128]{3,2,1,0:T(8,128)(2,1)S(1)} %bitcast.5, ...), custom_call_target="tpu_custom_call" | custom-call | flops 4000000000 | bytes 20000000 | tf_op jit(solution)/shard_map/pallas_call | solution.py:941
  65.9 2.0 %shard_map.123 = (bf16[8,16,64,128]{3,2,1,0:T(8,128)(2,1)}, f32[16,4,8,8,32]{4,3,2,1,0:T(8,128)}) custom-call(bf16[8,12,64,128]{3,2,1,0:T(8,128)(2,1)S(1)} %get-tuple-element.10.done_ref, f32[8,4,64,128]{3,2,1,0:T(8,128)S(1)} %get-tuple-element.11.rest_ref, bf16[16,1,16,128]{3,2,1,0:T(8,128)(2,1)S(1)} %get-tuple-element.12.cells_ref, ...), custom_call_target="tpu_custom_call" | custom-call | flops 1000000000 | bytes 10000000 | tf_op jit(solution)/shard_map/pallas_call | solution.py:967
Async XLA Ops:
  0.6 1.6 %copy-start = (bf16[1,8,16,64,128]{4,3,2,1,0:T(8,128)(2,1)S(1)}, bf16[1,8,16,64,128]{4,3,2,1,0:T(8,128)(2,1)}, u32[]{:S(2)}) copy-start(bf16[1,8,16,64,128]{4,3,2,1,0:T(8,128)(2,1)} %param.11) | copy-start | bytes 6291460

commit v6 on v5

--- a/solution.py
+++ b/solution.py
@@ -397,7 +397,7 @@
             ]
         )
     ]
-    for load in loads:
+    for load in loads[:3]:
         load.start()
 
     barrier = pltpu.get_barrier_semaphore()
@@ -605,6 +605,8 @@
 
     for load in loads[:3]:
         load.wait()
+    for load in loads[3:]:
+        load.start()
     for half in range(nh):
         blocks = []
         for q in range(hq):
@@ -785,16 +787,22 @@
     @pl.when(first)
     def _():
         forward(5, range(nh))
-        for half in range(nh):
+        for half in range(nh - 1):
             land(5, half)
 
-    for half in range(nh):
-        for q in range(hq if half < nh - 1 else hq - 1):
+    for half in range(nh - 1):
+        for q in range(hq):
             field = to_field(e, half, q)
             x0 = (half * hq + q) * xq
             for k in range(xq):
                 out[:, x0 + k] = (row(field, k) + u[:, x0 + k]).astype(bf16)
-    cells_ref[...] = r_ref[e, nh - 1, :, hq - 1 :]
+
+    @pl.when(first)
+    def _():
+        land(5, nh - 1)
+        rest_ref[:, : late - tail] = u[:, tail:late]
+
+    cells_ref[...] = r_ref[e, nh - 1]
 
     @pl.when(first)
     def _():
@@ -811,14 +819,14 @@
                 incoming = u[i, x] + blend(mix1, signals, i, True)
                 here.append(incoming.astype(bf16).astype(f32) * slope[i, x])
             for o in range(channels):
-                rest_ref[o, k] = blend(mix_ref, here, o, True)
+                rest_ref[o, late - tail + k] = blend(mix_ref, here, o, True)
             return carry
 
         lax.fori_loop(0, xq, step, 0)
 
     @pl.when(last)
     def _():
-        rest_ref[...] = u[:, late:]
+        rest_ref[...] = u[:, tail:]
 
     for half in range(nh):
         sent(0, half)
@@ -874,6 +882,10 @@
         stores.append(store)
     for store in stores:
         store.wait()
+
+
+def in_hbm(value):
+    return pltpu.with_memory_space_constraint(jnp.asarray(value), pltpu.HBM)
 
 
 def two_section_body(activations, cotangent, spectral_weights, pointwise, channel_bias):
@@ -914,8 +926,8 @@
     hbm = pl.BlockSpec(memory_space=pl.ANY)
     dma = pltpu.SemaphoreType.DMA
     grid = inputs.shape
-    done = grid[:1] + (xr - xq,) + grid[2:]
-    left = grid[:1] + (xq,) + grid[2:]
+    done = grid[:1] + ((nh - 1) * hq * xq,) + grid[2:]
+    left = grid[:1] + (hq * xq,) + grid[2:]
     scratch = [
         pltpu.VMEM(grid, bf16), pltpu.VMEM(grid, bf16), pltpu.VMEM(grid, bf16),
         pltpu.VMEM(weights.shape, f32),
@@ -943,7 +955,7 @@
         out_shape=(
             jax.ShapeDtypeStruct(done, bf16),
             jax.ShapeDtypeStruct(left, f32),
-            jax.ShapeDtypeStruct((n, 1, 16, lanes), bf16),
+            jax.ShapeDtypeStruct((n, hq, 16, lanes), bf16),
             pltpu.VMEM(weights.shape, f32),
             jax.ShapeDtypeStruct((2, rows, ny * lanes), bf16),
             jax.ShapeDtypeStruct((3 * nx * 16, xq * zr), bf16),
@@ -958,11 +970,9 @@
             flops=4 * 10**9, bytes_accessed=2 * 10**7, transcendentals=10**7
         ),
     )(
-        inputs, cotangent, weights, mixing, channel_bias,
-        *[
-            pltpu.with_memory_space_constraint(jnp.asarray(table), pltpu.HBM)
-            for table in [mixing, channel_bias] + tables
-        ],
+        *[in_hbm(v) for v in (inputs, cotangent, weights)],
+        mixing, channel_bias,
+        *[in_hbm(v) for v in [mixing, channel_bias] + tables],
     )
     input_grad, weight_grad = pl.pallas_call(
         functools.partial(finish_kernel, nx, ny, xq),
@@ -972,7 +982,7 @@
         ),
         in_specs=[vmem] * 6,
         out_specs=(hbm, hbm),
-        scratch_shapes=[pltpu.VMEM(left, bf16), dma((3,))],
+        scratch_shapes=[pltpu.VMEM(left, bf16), dma((2 + hq,))],
         compiler_params=pltpu.CompilerParams(vmem_limit_bytes=24 * 2**20),
         cost_estimate=pl.CostEstimate(flops=10**9, bytes_accessed=10**7, transcendentals=0),
     )(*parts)

time: 69.1 us -> 66.5 us (0.962); the launches traced: 68.1 us -> 66.3 us
  local copies, waits for them, and re-layouts: 1.58 us -> 0 us
    unnamed x2 -> x0, local copies, waits for them, and re-layouts: 1.58 us -> none
where the time goes in v6:
time: 66.5 us; the launch traced here: 66.3 us
  Pallas kernels  65.5 us (98%)
  between operations  0.82 us (1%)
    pallas_call x1, Pallas kernels, two_section_body(): pl.pallas_call(functools.partial(relay_kernel, nx, ny, xq, (3, 9, 12)), o...  63.4 us
    pallas_call x1, Pallas kernels, two_section_body(): pl.pallas_call(functools.partial(finish_kernel, nx, ny, xq), out_shape=(j...  2.16 us

profile of v6, /device:TPU:0, one launch (start us, length us, event | category | flops | bytes accessed | tf_op | source)
XLA Modules:
  0.0 66.3 jit_solution(14835990565196966247)
XLA Ops:
  0.6 63.4 %shard_map.122 = (bf16[8,8,64,128]{3,2,1,0:T(8,128)(2,1)S(1)}, f32[8,8,64,128]{3,2,1,0:T(8,128)S(1)}, bf16[16,2,16,128]{3,2,1,0:T(8,128)(2,1)S(1)}, f32[16,4,8,8...) custom-call(bf16[8,16,64,128]{3,2,1,0:T(8,128)(2,1)} %bitcast.5, ...), custom_call_target="tpu_custom_call" | custom-call | flops 4000000000 | bytes 20000000 | tf_op jit(solution)/shard_map/pallas_call | solution.py:953
  64.0 2.2 %shard_map.123 = (bf16[8,16,64,128]{3,2,1,0:T(8,128)(2,1)}, f32[16,4,8,8,32]{4,3,2,1,0:T(8,128)}) custom-call(bf16[8,8,64,128]{3,2,1,0:T(8,128)(2,1)S(1)} %get-tuple-element.10.done_ref, f32[8,8,64,128]{3,2,1,0:T(8,128)S(1)} %get-tuple-element.11.rest_ref, bf16[16,2,16,128]{3,2,1,0:T(8,128)(2,1)S(1)} %get-tuple-element.12.cells_ref, ...), custom_call_target="tpu_custom_call" | custom-call | flops 1000000000 | bytes 10000000 | tf_op jit(solution)/shard_map/pallas_call | solution.py:977

commit v7 on v6

--- a/solution.py
+++ b/solution.py
@@ -372,7 +372,7 @@
     u, v, slope, sig, in_modes, grad_modes, m_ref, mt_send, mt_recv,
     mixv1, biasv1, mix1, bias1, s_ref, p_ref, r_ref,
     load_sem, send_sem, recv_sem, row_send, row_recv, small_send, small_recv, store_sem,
-    tail_send, tail_recv, pair_send, pair_recv,
+    tail_send, tail_recv, pair_send, pair_recv, across_send,
 ):
     channels, xr, yr, zr = act.shape
     n = nx * ny
@@ -464,6 +464,18 @@
         lax.fori_loop(1, nx, begin, 0)
         r_ref[e, half, mine] = source(gx)[...]
 
+    def send_across(half):
+        def begin(k, carry):
+            d = lax.rem(gx + k, nx)
+            pltpu.make_async_remote_copy(
+                src_ref=p_ref.at[1, half, d], dst_ref=r_ref.at[3, half, mine],
+                send_sem=across_send.at[half], recv_sem=recv_sem.at[3, half],
+                device_id={"segment": 0, "gx": d}, device_id_type=mesh_ids,
+            ).start()
+            return carry
+
+        lax.fori_loop(0, nx, begin, 0)
+
     def pair_copy(e, half):
         block = r_ref.at[e, half, pl.ds(gy * nx, nx)]
         return pltpu.make_async_remote_copy(
@@ -476,6 +488,10 @@
         for half in halves:
             await_block(r_ref.at[e, half, pl.ds(0, nx - 1)], recv_sem.at[e, half])
             pair_copy(e, half).start()
+
+    def forward_across(half):
+        await_block(r_ref.at[3, half, pl.ds(0, nx)], recv_sem.at[3, half])
+        pair_copy(3, half).start()
 
     def land(e, half):
         await_block(r_ref.at[e, half, pl.ds(0, nx)], pair_recv.at[e, half])
@@ -535,13 +551,19 @@
             own = term if own is None else own + term
         return own.T.reshape(jl, channels, cl * MODES)
 
+    def spread(mt, k, half):
+        top, rest = split(mt)
+        table = [sp[i, half].reshape(nx * hq * 16, cl * MODES) for i in range(2)]
+        cells = dot(table[0], top) + dot(table[1], top) + dot(table[0], rest)
+        p_ref[k, half] = cells.astype(bf16).reshape(nx, hq, 16, lanes)
+
+    def send_spread(k, e, half):
+        send_along(lambda d: p_ref.at[k, half, d], e, half)
+
     def send_cells(mt, k, e, halves):
-        top, rest = split(mt)
         for half in halves:
-            table = [sp[i, half].reshape(nx * hq * 16, cl * MODES) for i in range(2)]
-            cells = dot(table[0], top) + dot(table[1], top) + dot(table[0], rest)
-            p_ref[k, half] = cells.astype(bf16).reshape(nx, hq, 16, lanes)
-            send_along(lambda d: p_ref.at[k, half, d], e, half)
+            spread(mt, k, half)
+            send_spread(k, e, half)
 
     def mixed():
         return m_ref[...].reshape(lanes, cl * MODES).T
@@ -675,9 +697,13 @@
 
         mix_back(2, lambda half: arrive(2, half))
         mt_send[1] = mixed()
-        modes_copy(1).start()
+        for half in range(nh - 1):
+            spread(mt_send[1], 1, half)
+            send_across(half)
         send_rows(cuts[1], cuts[2])
-        send_cells(mt_send[1], 1, 3, reversed(range(nh)))
+        spread(mt_send[1], 1, nh - 1)
+        for half in reversed(range(nh)):
+            send_spread(1, 3, half)
 
         blend_back(0, xr)
         for x in range(tail, xr):
@@ -697,6 +723,7 @@
         land(3, nh - 1)
         to_modes([packed(back_block(nh - 1, q, u)) for q in range(hq)], 2, nh - 1)
         lax.fori_loop(0, n, send_tail, 0)
+        send_across(nh - 1)
         send_rows(cuts[2], xr)
 
     def ahead_quarter(half, q):
@@ -742,18 +769,14 @@
         for half in range(nh - 1):
             for q in range(hq):
                 ahead_quarter(half, q)
-        modes_copy(1).wait_recv()
-        send_cells(mt_recv[1], 2, 3, range(nh))
-        forward(3, range(nh))
         for half in range(nh - 1):
+            forward_across(half)
             land(3, half)
             to_modes([packed(kept(back_block(half, q, v))) for q in range(hq)], 1, half)
             send_modes(1, 4, half)
         blend_back(0, tail)
-        land(3, nh - 1)
         for q in range(hq - 1):
             ahead_quarter(nh - 1, q)
-            kept(back_block(nh - 1, q, v))
 
         def await_half(half):
             if half < nh - 1:
@@ -763,6 +786,10 @@
 
         mix_back(4, await_half)
         send_cells(mixed(), 3, 5, range(nh))
+        forward_across(nh - 1)
+        land(3, nh - 1)
+        for q in range(hq - 1):
+            kept(back_block(nh - 1, q, v))
         if hq > 1:
             blend_back(tail, late)
         for target, e in ((v, 2), (u, 3)):
@@ -831,7 +858,7 @@
     for half in range(nh):
         sent(0, half)
         sent_along(1, half)
-        sent_along(3, half)
+        await_block(r_ref.at[3, half, pl.ds(0, nx)], pair_send.at[3, half])
     for copy in small:
         copy.wait_send()
     modes_copy(0).wait_send()
@@ -850,8 +877,9 @@
     def _():
         for half in range(nh):
             sent(2, half)
+            await_block(r_ref.at[3, half, pl.ds(0, nx - 1)], send_sem.at[3, half])
+            await_block(r_ref.at[3, half, pl.ds(0, nx)], across_send.at[half])
         sent_along(5, nh - 1)
-        modes_copy(1).wait_send()
         await_block(r_ref.at[4, nh - 1], tail_send.at[0])
         for x in range(xr):
             row_copy(x).wait_send()
@@ -948,7 +976,7 @@
         pltpu.VMEM((4, nh, nx, hq, 16, lanes), bf16),
         pltpu.VMEM((6, nh, n, hq, 16, lanes), bf16),
         dma((9,)), dma((6, nh)), dma((6, nh)),
-        dma((xr,)), dma((xr,)), dma((4,)), dma((4,)), dma((2,)), dma((1,)), dma((1,)), dma((6, nh)), dma((6, nh)),
+        dma((xr,)), dma((xr,)), dma((4,)), dma((4,)), dma((2,)), dma((1,)), dma((1,)), dma((6, nh)), dma((6, nh)), dma((nh,)),
     ]
     parts = pl.pallas_call(
         functools.partial(relay_kernel, nx, ny, xq, (3, 9, 12)),

time: 66.5 us -> 68.1 us (1.024)
  Pallas kernels: 65.5 us -> 67.1 us
    pallas_call x1, Pallas kernels: 63.4 us -> 65 us  [two_section_body(): pl.pallas_call(functools.partial(relay_kernel, nx, ny, xq, (3, 9, 12)), o...]
where the time goes in v7:
time: 68.1 us; the launch traced here: 67.9 us
  Pallas kernels  67.1 us (99%)
  between operations  0.82 us (1%)
    pallas_call x1, Pallas kernels, two_section_body(): pl.pallas_call(functools.partial(relay_kernel, nx, ny, xq, (3, 9, 12)), o...  65 us
    pallas_call x1, Pallas kernels, two_section_body(): pl.pallas_call(functools.partial(finish_kernel, nx, ny, xq), out_shape=(j...  2.16 us

profile of v7, /device:TPU:0, one launch (start us, length us, event | category | flops | bytes accessed | tf_op | source)
XLA Modules:
  0.0 67.9 jit_solution(8416990931926685895)
XLA Ops:
  0.6 65.0 %shard_map.122 = (bf16[8,8,64,128]{3,2,1,0:T(8,128)(2,1)S(1)}, f32[8,8,64,128]{3,2,1,0:T(8,128)S(1)}, bf16[16,2,16,128]{3,2,1,0:T(8,128)(2,1)S(1)}, f32[16,4,8,8...) custom-call(bf16[8,16,64,128]{3,2,1,0:T(8,128)(2,1)} %bitcast.5, ...), custom_call_target="tpu_custom_call" | custom-call | flops 4000000000 | bytes 20000000 | tf_op jit(solution)/shard_map/pallas_call | solution.py:981
  65.6 2.2 %shard_map.123 = (bf16[8,16,64,128]{3,2,1,0:T(8,128)(2,1)}, f32[16,4,8,8,32]{4,3,2,1,0:T(8,128)}) custom-call(bf16[8,8,64,128]{3,2,1,0:T(8,128)(2,1)S(1)} %get-tuple-element.10.done_ref, f32[8,8,64,128]{3,2,1,0:T(8,128)S(1)} %get-tuple-element.11.rest_ref, bf16[16,2,16,128]{3,2,1,0:T(8,128)(2,1)S(1)} %get-tuple-element.12.cells_ref, ...), custom_call_target="tpu_custom_call" | custom-call | flops 1000000000 | bytes 10000000 | tf_op jit(solution)/shard_map/pallas_call | solution.py:1005

commit v8 on v7

--- a/solution.py
+++ b/solution.py
@@ -623,7 +623,7 @@
 
     @pl.when(first)
     def _():
-        send_rows(tail, xr)
+        send_rows(tail, tail + cuts[0])
 
     for load in loads[:3]:
         load.wait()
@@ -670,6 +670,10 @@
     @pl.when(last)
     def _():
         send_rows(cuts[0], cuts[1])
+
+    @pl.when(first)
+    def _():
+        send_rows(tail + cuts[0], xr)
 
     send_cells(mt_send[0], 0, 1, range(nh))
 
@@ -690,10 +694,17 @@
                 blocks.append(jnp.concatenate(block, axis=1))
             to_modes(blocks, 1, half)
             send_modes(1, 2, half)
-
-        modes_copy(0).wait_recv()
-        send_cells(mt_recv[0], 3, 5, [nh - 1])
+            if half == 0:
+                modes_copy(0).wait_recv()
+                send_cells(mt_recv[0], 3, 5, [nh - 1])
+
         fetch_small()
+        forward(5, [nh - 1])
+        land(5, nh - 1)
+        for q in range(hq):
+            field = to_field(5, nh - 1, q)
+            for k in range(xq):
+                v[:, tail + q * xq + k] = row(field, k)
 
         mix_back(2, lambda half: arrive(2, half))
         mt_send[1] = mixed()
@@ -705,26 +716,24 @@
         for half in reversed(range(nh)):
             send_spread(1, 3, half)
 
-        blend_back(0, xr)
-        for x in range(tail, xr):
+        blend_back(tail, xr)
+
+        def step(x, carry):
             row_copy(x).wait_recv()
-        forward(5, [nh - 1])
-        land(5, nh - 1)
-        for q in range(hq):
-            field = to_field(5, nh - 1, q)
-            x0 = tail + q * xq
-            for k in range(xq):
-                values = [act1[i, x0 + k].astype(f32) for i in range(channels)]
-                here = row(field, k)
-                for o in range(channels):
-                    pre = here[o] + blend(mix1, values, o, False) + bias1[0, o]
-                    slope[o, x0 + k] = slope_of(pre)
+            values = [act1[i, x].astype(f32) for i in range(channels)]
+            for o in range(channels):
+                pre = v[o, x] + blend(mix1, values, o, False) + bias1[0, o]
+                slope[o, x] = slope_of(pre)
+            return carry
+
+        lax.fori_loop(tail, xr, step, 0)
         forward(3, reversed(range(nh)))
         land(3, nh - 1)
         to_modes([packed(back_block(nh - 1, q, u)) for q in range(hq)], 2, nh - 1)
         lax.fori_loop(0, n, send_tail, 0)
         send_across(nh - 1)
         send_rows(cuts[2], xr)
+        blend_back(0, tail)
 
     def ahead_quarter(half, q):
         field = to_field(2, half, q)

time: 68.1 us -> 67 us (0.984)
  Pallas kernels: 67.1 us -> 66 us
    pallas_call x1, Pallas kernels: 65 us -> 63.9 us  [two_section_body(): pl.pallas_call(functools.partial(relay_kernel, nx, ny, xq, (3, 9, 12)), o...]
where the time goes in v8:
time: 67 us; the launch traced here: 66.8 us
  Pallas kernels  66 us (99%)
  between operations  0.82 us (1%)
    pallas_call x1, Pallas kernels, two_section_body(): pl.pallas_call(functools.partial(relay_kernel, nx, ny, xq, (3, 9, 12)), o...  63.9 us
    pallas_call x1, Pallas kernels, two_section_body(): pl.pallas_call(functools.partial(finish_kernel, nx, ny, xq), out_shape=(j...  2.15 us

profile of v8, /device:TPU:0, one launch (start us, length us, event | category | flops | bytes accessed | tf_op | source)
XLA Modules:
  0.0 66.8 jit_solution(11069957399922927489)
XLA Ops:
  0.6 63.9 %shard_map.122 = (bf16[8,8,64,128]{3,2,1,0:T(8,128)(2,1)S(1)}, f32[8,8,64,128]{3,2,1,0:T(8,128)S(1)}, bf16[16,2,16,128]{3,2,1,0:T(8,128)(2,1)S(1)}, f32[16,4,8,8...) custom-call(bf16[8,16,64,128]{3,2,1,0:T(8,128)(2,1)} %bitcast.5, ...), custom_call_target="tpu_custom_call" | custom-call | flops 4000000000 | bytes 20000000 | tf_op jit(solution)/shard_map/pallas_call | solution.py:990
  64.5 2.2 %shard_map.123 = (bf16[8,16,64,128]{3,2,1,0:T(8,128)(2,1)}, f32[16,4,8,8,32]{4,3,2,1,0:T(8,128)}) custom-call(bf16[8,8,64,128]{3,2,1,0:T(8,128)(2,1)S(1)} %get-tuple-element.10.done_ref, f32[8,8,64,128]{3,2,1,0:T(8,128)S(1)} %get-tuple-element.11.rest_ref, bf16[16,2,16,128]{3,2,1,0:T(8,128)(2,1)S(1)} %get-tuple-element.12.cells_ref, ...), custom_call_target="tpu_custom_call" | custom-call | flops 1000000000 | bytes 10000000 | tf_op jit(solution)/shard_map/pallas_call | solution.py:1014

commit v9 on v8

--- a/solution.py
+++ b/solution.py
@@ -538,6 +538,30 @@
     def row(field, x):
         return field[:, x * zr : (x + 1) * zr].reshape(channels, yr, zr)
 
+    def stash(e, half, target):
+        def step(q, carry):
+            field = to_field(e, half, q)
+            x0 = (half * hq + q) * xq
+            for k in range(xq):
+                target[:, x0 + k] = row(field, k)
+            return carry
+
+        lax.fori_loop(0, hq, step, 0)
+
+    def ahead_rows(start, stop):
+        def step(x, carry):
+            row_copy(x).wait_recv()
+            values = [act1[i, x].astype(f32) for i in range(channels)]
+            signals = []
+            for o in range(channels):
+                pre = v[o, x] + blend(mix1, values, o, False) + bias1[0, o]
+                signals.append(cot[o, x].astype(f32) * slope_of(pre))
+            for i in range(channels):
+                v[i, x] = blend(mix1, signals, i, True)
+            return carry
+
+        lax.fori_loop(start, stop, step, 0)
+
     def send_modes(k, e, half):
         send_half(lambda d, h: s_ref.at[k, half, h * nx + d], e, half)
 
@@ -682,15 +706,17 @@
         forward(1, range(nh))
         for half in range(nh):
             land(1, half)
+            stash(1, half, sig)
+
+            def step(x, carry):
+                sig[:, x] = cot[:, x].astype(f32) * slope_of(sig[:, x] + u[:, x])
+                return carry
+
+            lax.fori_loop(half * hq * xq, (half + 1) * hq * xq, step, 0)
             blocks = []
             for q in range(hq):
-                field = to_field(1, half, q)
                 x0 = (half * hq + q) * xq
-                block = []
-                for k in range(xq):
-                    signal = cot[:, x0 + k].astype(f32) * slope_of(row(field, k) + u[:, x0 + k])
-                    sig[:, x0 + k] = signal
-                    block.append(signal.astype(bf16).reshape(rows, zr))
+                block = [sig[:, x0 + k].astype(bf16).reshape(rows, zr) for k in range(xq)]
                 blocks.append(jnp.concatenate(block, axis=1))
             to_modes(blocks, 1, half)
             send_modes(1, 2, half)
@@ -701,10 +727,7 @@
         fetch_small()
         forward(5, [nh - 1])
         land(5, nh - 1)
-        for q in range(hq):
-            field = to_field(5, nh - 1, q)
-            for k in range(xq):
-                v[:, tail + q * xq + k] = row(field, k)
+        stash(5, nh - 1, v)
 
         mix_back(2, lambda half: arrive(2, half))
         mt_send[1] = mixed()
@@ -735,20 +758,6 @@
         send_rows(cuts[2], xr)
         blend_back(0, tail)
 
-    def ahead_quarter(half, q):
-        field = to_field(2, half, q)
-        x0 = (half * hq + q) * xq
-        for k in range(xq):
-            row_copy(x0 + k).wait_recv()
-            values = [act1[i, x0 + k].astype(f32) for i in range(channels)]
-            here = row(field, k)
-            signals = []
-            for o in range(channels):
-                pre = here[o] + blend(mix1, values, o, False) + bias1[0, o]
-                signals.append(cot[o, x0 + k].astype(f32) * slope_of(pre))
-            for i in range(channels):
-                v[i, x0 + k] = blend(mix1, signals, i, True)
-
     def kept(block):
         for x, signal in block:
             sig[:, x] = signal
@@ -762,30 +771,28 @@
         forward(1, range(nh))
         for half in range(nh):
             land(1, half)
-
-            def step(q, carry):
-                field = to_field(1, half, q)
-                x0 = (half * hq + q) * xq
-                for k in range(xq):
-                    slope[:, x0 + k] = slope_of(row(field, k) + u[:, x0 + k])
+            stash(1, half, slope)
+
+            def step(x, carry):
+                slope[:, x] = slope_of(slope[:, x] + u[:, x])
                 return carry
 
-            lax.fori_loop(0, hq, step, 0)
+            lax.fori_loop(half * hq * xq, (half + 1) * hq * xq, step, 0)
 
         forward(2, range(nh))
         for half in range(nh):
             land(2, half)
         for half in range(nh - 1):
-            for q in range(hq):
-                ahead_quarter(half, q)
+            stash(2, half, v)
+        ahead_rows(0, tail)
         for half in range(nh - 1):
             forward_across(half)
             land(3, half)
             to_modes([packed(kept(back_block(half, q, v))) for q in range(hq)], 1, half)
             send_modes(1, 4, half)
         blend_back(0, tail)
-        for q in range(hq - 1):
-            ahead_quarter(nh - 1, q)
+        stash(2, nh - 1, v)
+        ahead_rows(tail, late)
 
         def await_half(half):
             if half < nh - 1:
@@ -801,10 +808,9 @@
             kept(back_block(nh - 1, q, v))
         if hq > 1:
             blend_back(tail, late)
-        for target, e in ((v, 2), (u, 3)):
-            field = to_field(e, nh - 1, hq - 1)
-            for k in range(xq):
-                target[:, late + k] = row(field, k)
+        field = to_field(3, nh - 1, hq - 1)
+        for k in range(xq):
+            u[:, late + k] = row(field, k)
 
     def weight_grad(j, carry):
         for c in range(cl):
@@ -826,12 +832,13 @@
         for half in range(nh - 1):
             land(5, half)
 
-    for half in range(nh - 1):
-        for q in range(hq):
-            field = to_field(e, half, q)
-            x0 = (half * hq + q) * xq
-            for k in range(xq):
-                out[:, x0 + k] = (row(field, k) + u[:, x0 + k]).astype(bf16)
+    def finish(q, carry):
+        field = to_field(e, q // hq, lax.rem(q, hq))
+        for k in range(xq):
+            out[:, q * xq + k] = (row(field, k) + u[:, q * xq + k]).astype(bf16)
+        return carry
+
+    lax.fori_loop(0, (nh - 1) * hq, finish, 0)
 
     @pl.when(first)
     def _():
@@ -988,7 +995,7 @@
         dma((xr,)), dma((xr,)), dma((4,)), dma((4,)), dma((2,)), dma((1,)), dma((1,)), dma((6, nh)), dma((6, nh)), dma((nh,)),
     ]
     parts = pl.pallas_call(
-        functools.partial(relay_kernel, nx, ny, xq, (3, 9, 12)),
+        functools.partial(relay_kernel, nx, ny, xq, (4, 10, 12)),
         out_shape=(
             jax.ShapeDtypeStruct(done, bf16),
             jax.ShapeDtypeStruct(left, f32),

time: 67 us -> 67.4 us (level)
  no operation moved by 1% of the time
where the time goes in v9:
time: 67.4 us; the launch traced here: 67.2 us
  Pallas kernels  66.4 us (99%)
  between operations  0.8 us (1%)
    pallas_call x1, Pallas kernels, two_section_body(): pl.pallas_call(functools.partial(relay_kernel, nx, ny, xq, (4, 10, 12)),...  64.3 us
    pallas_call x1, Pallas kernels, two_section_body(): pl.pallas_call(functools.partial(finish_kernel, nx, ny, xq), out_shape=(j...  2.15 us

profile of v9, /device:TPU:0, one launch (start us, length us, event | category | flops | bytes accessed | tf_op | source)
XLA Modules:
  0.0 67.2 jit_solution(15055552531106910590)
XLA Ops:
  0.6 64.3 %shard_map.122 = (bf16[8,8,64,128]{3,2,1,0:T(8,128)(2,1)S(1)}, f32[8,8,64,128]{3,2,1,0:T(8,128)S(1)}, bf16[16,2,16,128]{3,2,1,0:T(8,128)(2,1)S(1)}, f32[16,4,8,8...) custom-call(bf16[8,16,64,128]{3,2,1,0:T(8,128)(2,1)} %bitcast.5, ...), custom_call_target="tpu_custom_call" | custom-call | flops 4000000000 | bytes 20000000 | tf_op jit(solution)/shard_map/pallas_call | solution.py:997
  64.9 2.2 %shard_map.123 = (bf16[8,16,64,128]{3,2,1,0:T(8,128)(2,1)}, f32[16,4,8,8,32]{4,3,2,1,0:T(8,128)}) custom-call(bf16[8,8,64,128]{3,2,1,0:T(8,128)(2,1)S(1)} %get-tuple-element.10.done_ref, f32[8,8,64,128]{3,2,1,0:T(8,128)S(1)} %get-tuple-element.11.rest_ref, bf16[16,2,16,128]{3,2,1,0:T(8,128)(2,1)S(1)} %get-tuple-element.12.cells_ref, ...), custom_call_target="tpu_custom_call" | custom-call | flops 1000000000 | bytes 10000000 | tf_op jit(solution)/shard_map/pallas_call | solution.py:1021

commit v10 on v6

--- a/solution.py
+++ b/solution.py
@@ -601,7 +601,7 @@
 
     @pl.when(first)
     def _():
-        send_rows(tail, xr)
+        send_rows(tail, tail + cuts[0])
 
     for load in loads[:3]:
         load.wait()
@@ -648,6 +648,10 @@
     @pl.when(last)
     def _():
         send_rows(cuts[0], cuts[1])
+
+    @pl.when(first)
+    def _():
+        send_rows(tail + cuts[0], xr)
 
     send_cells(mt_send[0], 0, 1, range(nh))
 
@@ -680,14 +684,13 @@
         send_cells(mt_send[1], 1, 3, reversed(range(nh)))
 
         blend_back(0, xr)
-        for x in range(tail, xr):
-            row_copy(x).wait_recv()
         forward(5, [nh - 1])
         land(5, nh - 1)
         for q in range(hq):
             field = to_field(5, nh - 1, q)
             x0 = tail + q * xq
             for k in range(xq):
+                row_copy(x0 + k).wait_recv()
                 values = [act1[i, x0 + k].astype(f32) for i in range(channels)]
                 here = row(field, k)
                 for o in range(channels):
@@ -755,6 +758,11 @@
             ahead_quarter(nh - 1, q)
             kept(back_block(nh - 1, q, v))
 
+        for target, e in ((v, 2), (u, 3)):
+            field = to_field(e, nh - 1, hq - 1)
+            for k in range(xq):
+                target[:, late + k] = row(field, k)
+
         def await_half(half):
             if half < nh - 1:
                 arrive(4, half)
@@ -765,10 +773,6 @@
         send_cells(mixed(), 3, 5, range(nh))
         if hq > 1:
             blend_back(tail, late)
-        for target, e in ((v, 2), (u, 3)):
-            field = to_field(e, nh - 1, hq - 1)
-            for k in range(xq):
-                target[:, late + k] = row(field, k)
 
     def weight_grad(j, carry):
         for c in range(cl):

time: 66.5 us -> 66.4 us (level)
  no operation moved by 1% of the time
where the time goes in v10:
time: 66.4 us; the launch traced here: 66.2 us
  Pallas kernels  65.4 us (98%)
  between operations  0.82 us (1%)
    pallas_call x1, Pallas kernels, two_section_body(): pl.pallas_call(functools.partial(relay_kernel, nx, ny, xq, (3, 9, 12)), o...  63.2 us
    pallas_call x1, Pallas kernels, two_section_body(): pl.pallas_call(functools.partial(finish_kernel, nx, ny, xq), out_shape=(j...  2.16 us

profile of v10, /device:TPU:0, one launch (start us, length us, event | category | flops | bytes accessed | tf_op | source)
XLA Modules:
  0.0 66.2 jit_solution(17401062700233026665)
XLA Ops:
  0.6 63.2 %shard_map.122 = (bf16[8,8,64,128]{3,2,1,0:T(8,128)(2,1)S(1)}, f32[8,8,64,128]{3,2,1,0:T(8,128)S(1)}, bf16[16,2,16,128]{3,2,1,0:T(8,128)(2,1)S(1)}, f32[16,4,8,8...) custom-call(bf16[8,16,64,128]{3,2,1,0:T(8,128)(2,1)} %bitcast.5, ...), custom_call_target="tpu_custom_call" | custom-call | flops 4000000000 | bytes 20000000 | tf_op jit(solution)/shard_map/pallas_call | solution.py:957
  63.9 2.2 %shard_map.123 = (bf16[8,16,64,128]{3,2,1,0:T(8,128)(2,1)}, f32[16,4,8,8,32]{4,3,2,1,0:T(8,128)}) custom-call(bf16[8,8,64,128]{3,2,1,0:T(8,128)(2,1)S(1)} %get-tuple-element.10.done_ref, f32[8,8,64,128]{3,2,1,0:T(8,128)S(1)} %get-tuple-element.11.rest_ref, bf16[16,2,16,128]{3,2,1,0:T(8,128)(2,1)S(1)} %get-tuple-element.12.cells_ref, ...), custom_call_target="tpu_custom_call" | custom-call | flops 1000000000 | bytes 10000000 | tf_op jit(solution)/shard_map/pallas_call | solution.py:981

commit v11 on v10

--- a/solution.py
+++ b/solution.py
@@ -564,10 +564,14 @@
     def fetch_small():
         for copy in small:
             copy.wait_recv()
-        for k, (source, target) in enumerate([(mixv1, mix1), (biasv1, bias1)]):
-            copy = pltpu.make_async_copy(source, target, store_sem.at[k])
-            copy.start()
-            copy.wait()
+        fetches = [
+            pltpu.make_async_copy(source, target, store_sem.at[k])
+            for k, (source, target) in enumerate([(mixv1, mix1), (biasv1, bias1)])
+        ]
+        for fetch in fetches:
+            fetch.start()
+        for fetch in fetches:
+            fetch.wait()
 
     def back_block(half, q, offset):
         field = to_field(3, half, q)
@@ -725,7 +729,6 @@
     def _():
         modes_copy(0).wait_recv()
         send_cells(mt_recv[0], 1, 2, range(nh))
-        fetch_small()
         forward(1, range(nh))
         for half in range(nh):
             land(1, half)
@@ -740,6 +743,7 @@
             lax.fori_loop(0, hq, step, 0)
 
         forward(2, range(nh))
+        fetch_small()
         for half in range(nh):
             land(2, half)
         for half in range(nh - 1):

time: 66.4 us -> 66.4 us (level)
  no operation moved by 1% of the time
where the time goes in v11:
time: 66.4 us; the launch traced here: 66.2 us
  Pallas kernels  65.4 us (98%)
  between operations  0.82 us (1%)
    pallas_call x1, Pallas kernels, two_section_body(): pl.pallas_call(functools.partial(relay_kernel, nx, ny, xq, (3, 9, 12)), o...  63.2 us
    pallas_call x1, Pallas kernels, two_section_body(): pl.pallas_call(functools.partial(finish_kernel, nx, ny, xq), out_shape=(j...  2.16 us

profile of v11, /device:TPU:0, one launch (start us, length us, event | category | flops | bytes accessed | tf_op | source)
XLA Modules:
  0.0 66.2 jit_solution(3043178464907942181)
XLA Ops:
  0.6 63.2 %shard_map.122 = (bf16[8,8,64,128]{3,2,1,0:T(8,128)(2,1)S(1)}, f32[8,8,64,128]{3,2,1,0:T(8,128)S(1)}, bf16[16,2,16,128]{3,2,1,0:T(8,128)(2,1)S(1)}, f32[16,4,8,8...) custom-call(bf16[8,16,64,128]{3,2,1,0:T(8,128)(2,1)} %bitcast.5, ...), custom_call_target="tpu_custom_call" | custom-call | flops 4000000000 | bytes 20000000 | tf_op jit(solution)/shard_map/pallas_call | solution.py:961
  63.9 2.2 %shard_map.123 = (bf16[8,16,64,128]{3,2,1,0:T(8,128)(2,1)}, f32[16,4,8,8,32]{4,3,2,1,0:T(8,128)}) custom-call(bf16[8,8,64,128]{3,2,1,0:T(8,128)(2,1)S(1)} %get-tuple-element.10.done_ref, f32[8,8,64,128]{3,2,1,0:T(8,128)S(1)} %get-tuple-element.11.rest_ref, bf16[16,2,16,128]{3,2,1,0:T(8,128)(2,1)S(1)} %get-tuple-element.12.cells_ref, ...), custom_call_target="tpu_custom_call" | custom-call | flops 1000000000 | bytes 10000000 | tf_op jit(solution)/shard_map/pallas_call | solution.py:985

commit v12 on v10

--- a/solution.py
+++ b/solution.py
@@ -780,7 +780,13 @@
             wgrad[j, c] = in_modes[j][:, None, part] * grad_modes[j][None, :, part]
         return carry
 
-    lax.fori_loop(0, jl, weight_grad, 0)
+    lax.fori_loop(0, jl // 2, weight_grad, 0)
+
+    @pl.when(first)
+    def _():
+        forward(5, range(nh))
+
+    lax.fori_loop(jl // 2, jl, weight_grad, 0)
     e = 3 + 2 * (1 - seg)
 
     @pl.when(last)
@@ -790,7 +796,6 @@
 
     @pl.when(first)
     def _():
-        forward(5, range(nh))
         for half in range(nh - 1):
             land(5, half)
 

time: 66.4 us -> 67.2 us (1.012)
  Pallas kernels: 65.4 us -> 66.2 us
    pallas_call x1, Pallas kernels: 63.2 us -> 64 us  [two_section_body(): pl.pallas_call(functools.partial(relay_kernel, nx, ny, xq, (3, 9, 12)), o...]
where the time goes in v12:
time: 67.2 us; the launch traced here: 67 us
  Pallas kernels  66.2 us (99%)
  between operations  0.82 us (1%)
    pallas_call x1, Pallas kernels, two_section_body(): pl.pallas_call(functools.partial(relay_kernel, nx, ny, xq, (3, 9, 12)), o...  64 us
    pallas_call x1, Pallas kernels, two_section_body(): pl.pallas_call(functools.partial(finish_kernel, nx, ny, xq), out_shape=(j...  2.16 us

profile of v12, /device:TPU:0, one launch (start us, length us, event | category | flops | bytes accessed | tf_op | source)
XLA Modules:
  0.0 67.0 jit_solution(5869329523236867381)
XLA Ops:
  0.6 64.0 %shard_map.122 = (bf16[8,8,64,128]{3,2,1,0:T(8,128)(2,1)S(1)}, f32[8,8,64,128]{3,2,1,0:T(8,128)S(1)}, bf16[16,2,16,128]{3,2,1,0:T(8,128)(2,1)S(1)}, f32[16,4,8,8...) custom-call(bf16[8,16,64,128]{3,2,1,0:T(8,128)(2,1)} %bitcast.5, ...), custom_call_target="tpu_custom_call" | custom-call | flops 4000000000 | bytes 20000000 | tf_op jit(solution)/shard_map/pallas_call | solution.py:962
  64.7 2.2 %shard_map.123 = (bf16[8,16,64,128]{3,2,1,0:T(8,128)(2,1)}, f32[16,4,8,8,32]{4,3,2,1,0:T(8,128)}) custom-call(bf16[8,8,64,128]{3,2,1,0:T(8,128)(2,1)S(1)} %get-tuple-element.10.done_ref, f32[8,8,64,128]{3,2,1,0:T(8,128)S(1)} %get-tuple-element.11.rest_ref, bf16[16,2,16,128]{3,2,1,0:T(8,128)(2,1)S(1)} %get-tuple-element.12.cells_ref, ...), custom_call_target="tpu_custom_call" | custom-call | flops 1000000000 | bytes 10000000 | tf_op jit(solution)/shard_map/pallas_call | solution.py:986
